TPU v7x, 512 devices: a whole 4x8x8 slice. The times are simulated.
512 devices in a mesh: dp: 32 (over y, z_hi, core), tensor: 16 (over z_lo, x).
Axes of the slice: x: 4, y: 8, z: 8 (z_hi: 2, z_lo: 4; z = z_hi * 4 + z_lo), core: 2. Of those that a mesh axis runs over, the one named last changes fastest.
Arguments:
- queries: bfloat16 [30720, 8192], P('dp', 'tensor'), may hold values from -6 to 6
- features: bfloat16 [32, 128, 7680], P('dp'), may hold values from -6 to 6
- key_weight: bfloat16 [7680, 1024], P('dp', 'tensor'), may hold values from -0.0625 to 0.0625
- value_weight: bfloat16 [7680, 1024], P('dp', 'tensor'), may hold values from -0.0625 to 0.0625
- query_gain: float32 [128], replicated, may hold values from 0.25 to 1.75
- key_gain: float32 [128], replicated, may hold values from 0.25 to 1.75
- out_grad: bfloat16 [30720, 8192], P('dp', 'tensor'), may hold values from -6 to 6
- tile_counts: int32 [32], P('dp'), may hold values from 1 to 4, as said below
Outputs:
- query_grad: bfloat16 [30720, 8192], P('dp', 'tensor')
- feature_grad: bfloat16 [32, 128, 7680], P('dp', None, 'tensor')
- key_weight_grad: float32 [7680, 1024], P('dp', 'tensor')
- value_weight_grad: float32 [7680, 1024], P('dp', 'tensor')
Inputs may be any that keep to these rules, and one draw needn't show every extreme that they name: Each sample's text attends to its first 32 * tile_counts image tokens; some sample has 4 tiles.
All inputs are finite; a program needn't handle non-finite values.
Results may differ from a plain program's by a relative error of at most 0.025.
Values may be sent and summed in bfloat16 or wider, within the bound.
A program may use at most 64 MiB of HBM per device.

v0:
```python
import math

import jax
import jax.numpy as jnp
from jax import lax
from jax.sharding import PartitionSpec as P

TILE_ROWS = 32


EPS = 1e-05


def swapped(shard, axis, bit):
    return lax.ppermute(shard, axis, [(i, i ^ 1 << bit) for i in range(lax.axis_size(axis))])


def norm_rows(inputs, gain):
    scaling = lax.rsqrt(jnp.mean(inputs * inputs, -1, keepdims=True) + EPS)
    return (inputs * scaling * gain, scaling)


def norm_back(inputs, scaling, gain, upstream):
    weighted = upstream * gain
    return scaling * weighted - inputs * scaling**3 * jnp.mean(weighted * inputs, -1, keepdims=True)


def attend_back(query_rows, upstream_rows, keys_pre, value_rows, tile_count, query_gain, key_gain):
    head_width = keys_pre.shape[1]
    inverse = 1.0 / math.sqrt(head_width)
    query_float = query_rows.astype(jnp.float32)
    normed_q, q_scaling = norm_rows(query_float, query_gain)
    query_bf = normed_q.astype(jnp.bfloat16)
    key_float = keys_pre.astype(jnp.float32)
    normed_k, k_scaling = norm_rows(key_float, key_gain)
    key_bf = normed_k.astype(jnp.bfloat16)
    scores = (
        jnp.einsum("thd,id->thi", query_bf, key_bf, preferred_element_type=jnp.float32) * inverse
    )
    live_keys = (jnp.arange(keys_pre.shape[0]) < tile_count * TILE_ROWS).astype(jnp.float32)
    exponent = jnp.exp(scores) * live_keys
    probabilities = exponent / jnp.sum(exponent, -1, keepdims=True)
    probs_bf = probabilities.astype(jnp.bfloat16)
    attended = jnp.einsum("thi,id->thd", probs_bf, value_rows, preferred_element_type=jnp.float32)
    row_delta = jnp.sum(upstream_rows.astype(jnp.float32) * attended, -1, keepdims=True)
    value_grad = jnp.einsum(
        "thi,thd->id", probs_bf, upstream_rows, preferred_element_type=jnp.float32
    )
    prob_grad = jnp.einsum(
        "thd,id->thi", upstream_rows, value_rows, preferred_element_type=jnp.float32
    )
    score_grad = (probabilities * (prob_grad - row_delta)).astype(jnp.bfloat16)
    normed_q_grad = (
        jnp.einsum("thi,id->thd", score_grad, key_bf, preferred_element_type=jnp.float32) * inverse
    )
    normed_k_grad = (
        jnp.einsum("thi,thd->id", score_grad, query_bf, preferred_element_type=jnp.float32)
        * inverse
    )
    query_grad = norm_back(query_float, q_scaling, query_gain, normed_q_grad).astype(jnp.bfloat16)
    key_grad = norm_back(key_float, k_scaling, key_gain, normed_k_grad)
    return (query_grad, key_grad, value_grad)


def split_halves(key_part, value_part, low_side, column_half):
    key_first, key_second = (key_part[:, :column_half], key_part[:, column_half:])
    value_first, value_second = (value_part[:, :column_half], value_part[:, column_half:])
    own_part = jnp.concatenate(
        (
            jnp.where(low_side, key_first, key_second),
            jnp.where(low_side, value_first, value_second),
        ),
        1,
    )
    far_part = jnp.concatenate(
        (
            jnp.where(low_side, key_second, key_first),
            jnp.where(low_side, value_second, value_first),
        ),
        1,
    )
    return (own_part, far_part)


def shards(
    queries, features, key_weight, value_weight, query_gain, key_gain, out_grad, tile_counts
):
    samples, own_rows, feature_width = features.shape
    column_half = key_weight.shape[1]
    head_width = 2 * column_half
    rows_all = samples * own_rows
    flattened = features.reshape(rows_all, feature_width)
    stacked = jnp.concatenate((key_weight, value_weight), 1)
    low_side = lax.axis_index("tensor") % 2 == 0
    whole_weights = lax.all_gather(stacked, "dp", axis=0, tiled=True)
    projected = jnp.dot(flattened, whole_weights, preferred_element_type=jnp.float32)
    own_block = projected.astype(jnp.bfloat16)
    partner_block = swapped(own_block, "tensor", 0)
    first_half = jnp.where(low_side, own_block, partner_block)
    second_half = jnp.where(low_side, partner_block, own_block)
    keys_pre = jnp.concatenate((first_half[:, :column_half], second_half[:, :column_half]), 1)
    value_rows = jnp.concatenate((first_half[:, column_half:], second_half[:, column_half:]), 1)
    tokens = queries.shape[0]
    heads_dev = queries.shape[1] // head_width
    query_grad, key_grad, value_grad = attend_back(
        queries.reshape(tokens, heads_dev, head_width),
        out_grad.reshape(tokens, heads_dev, head_width),
        keys_pre,
        value_rows,
        tile_counts[0],
        query_gain,
        key_gain,
    )
    own_part, far_part = split_halves(key_grad, value_grad, low_side, column_half)
    summed = own_part + swapped(far_part.astype(jnp.bfloat16), "tensor", 0).astype(far_part.dtype)
    grads_sent = summed.astype(jnp.bfloat16)
    contract_cols = (((1,), (1,)), ((), ()))
    feature_term = lax.dot_general(
        grads_sent, whole_weights, contract_cols, preferred_element_type=jnp.float32
    )
    feature_grad = lax.psum_scatter(
        feature_term.reshape(samples, own_rows, feature_width).astype(jnp.bfloat16),
        "tensor",
        scatter_dimension=2,
        tiled=True,
    )
    weight_sum = lax.psum_scatter(
        lax.dot_general(
            flattened, grads_sent, (((0,), (0,)), ((), ())), preferred_element_type=jnp.float32
        ).astype(jnp.bfloat16),
        "dp",
        scatter_dimension=0,
        tiled=True,
    ).astype(jnp.float32)
    return (
        query_grad.reshape(tokens, heads_dev * head_width),
        feature_grad,
        weight_sum[:, :column_half],
        weight_sum[:, column_half:],
    )


def solution(mesh):
    placed = (
        P("dp", "tensor"),
        P("dp", None, None),
        P("dp", "tensor"),
        P("dp", "tensor"),
        P(),
        P(),
        P("dp", "tensor"),
        P("dp"),
    )
    return jax.shard_map(
        shards,
        mesh=mesh,
        in_specs=placed,
        out_specs=(
            P("dp", "tensor"),
            P("dp", None, "tensor"),
            P("dp", "tensor"),
            P("dp", "tensor"),
        ),
        check_vma=False,
    )
```

profile of v0, /device:TPU:8, one launch (start us, length us, event | category | flops | bytes accessed | tf_op | source)
XLA Modules:
  0.0 361.0 jit_solution(11499321945268197962)
XLA Ops:
  7.2 0.0 copy-start
  7.2 0.0 all-gather.2.cloned.1.call-start
  7.2 1.0 copy.65
  8.2 0.9 copy.66
  9.1 0.7 pad_maximum_fusion
  9.8 0.0 all-gather.2.cloned.1.call-update
  9.9 0.0 reduce-scatter.9.cloned.1.call-start
  10.6 2.8 reshape.72
  13.4 0.0 copy-start.3
  13.4 2.7 multiply_reduce_fusion.1
  16.1 0.2 copy.63
  16.2 0.0 copy-done.3
  16.3 0.0 copy-start.1
  16.3 0.0 copy-start.5
  16.3 92.7 %all-gather.2.cloned.1.call-done = bf16[7680,128]{1,0:T(8,128)(2,1)} async-done(((bf16[240,128]{1,0:T(8,128)(2,1)}), bf16[7680,128]{1,0:T(8,128)(2,1)}) %all-gather.2.cloned.1.call-update) | async-done | bytes 1966096 | tf_op jit(solution)/shard_map/all_gather | solution.py:95
  109.0 0.0 copy-done
  109.0 2.3 fusion.18
  111.3 3.4 collective-permute-start
  114.7 2.4 collective-permute-done
  117.2 0.0 copy-done.1
  117.2 0.0 copy-done.5
  117.2 0.0 copy-start.4
  117.2 1.4 fusion.13
  118.6 0.0 copy-done.4
  118.7 1.1 convolution_bitcast_fusion
  119.8 1.3 multiply_reduce_fusion
  121.1 1.4 fusion.8
  122.5 0.0 copy-start.2
  122.5 1.3 fusion.36
  123.8 3.4 collective-permute-start.1
  127.3 0.0 copy-done.2
  127.3 2.4 collective-permute-done.1
  129.7 1.9 fusion.1
  131.6 4.0 %copy.88 = bf16[7680,128]{1,0:T(8,128)(2,1)} copy(bf16[7680,128]{0,1:T(8,128)(2,1)} %fusion.1) | data formatting | bytes 3932160
  135.6 0.0 reduce-scatter.9.cloned.1.call-update
  135.6 0.0 reduce-scatter.7.cloned.1.call-start
  135.6 3.5 fusion
  139.2 8.9 %copy.86 = bf16[1,128,7680]{1,0,2:T(2,128)(2,1)} copy(bf16[1,128,7680]{2,1,0:T(8,128)(2,1)} %fusion) | data formatting | bytes 3932160
  148.0 3.7 %copy.118 = bf16[7680,1,128]{2,0,1:T(8,128)(2,1)} copy(bf16[7680,1,128]{2,1,0:T(2,128)(2,1)} %bitcast.105) | data formatting | bytes 3932160
  151.7 0.0 reduce-scatter.7.cloned.1.call-update
  151.8 2.1 fusion.7
  153.9 3.3 copy_bitcast_fusion.1
  157.1 105.8 %reduce-scatter.9.cloned.1.call-done = bf16[240,128]{1,0:T(8,128)(2,1)} async-done(((bf16[7680,128]{1,0:T(8,128)(2,1)}), bf16[240,128]{1,0:T(8,128)(2,1)}) %reduce-scatter.9.cloned.1.call-update) | async-done | bytes 61456
  263.0 0.9 copy.89
  263.9 0.7 fusion.48
  264.6 88.2 %reduce-scatter.7.cloned.1.call-done = bf16[480,128]{1,0:T(8,128)(2,1)} async-done(((bf16[7680,128]{1,0:T(8,128)(2,1)}), bf16[480,128]{1,0:T(8,128)(2,1)}) %reduce-scatter.7.cloned.1.call-update) | async-done | bytes 122896
  352.8 1.0 reshape_bitcast_fusion
  353.8 0.7 copy.77
  (15 shorter events, 0.2 us)
Async XLA Ops:
  7.2 101.9 %copy-start = (bf16[1,128,7680]{2,1,0:T(8,128)(2,1)S(1)}, bf16[1,128,7680]{2,1,0:T(8,128)(2,1)}, u32[]{:S(2)}) copy-start(bf16[1,128,7680]{2,1,0:T(8,128)(2,1)} %param.9) | copy-start | bytes 5898244
  7.2 101.9 %all-gather.2.cloned.1.call-start = ((), (), s32[]{:S(2)}) async-start(), calls=%async_computation.2 | async-start | bytes 2027520 | tf_op jit(solution)/shard_map/all_gather | solution.py:95
  9.9 253.1 %reduce-scatter.9.cloned.1.call-start = ((), (), s32[]{:S(2)}) async-start(), calls=%async_computation.4 | async-start | bytes 2027520
  13.4 2.9 copy-start.3
  16.3 100.9 %copy-start.1 = (bf16[960,512]{1,0:T(8,128)(2,1)S(1)}, bf16[960,512]{1,0:T(8,128)(2,1)}, u32[]{:S(2)}) copy-start(bf16[960,512]{1,0:T(8,128)(2,1)} %param.8) | copy-start | bytes 2949124
  16.3 100.9 %copy-start.5 = (f32[128]{0:T(128)S(1)}, f32[128]{0:T(128)}, u32[]{:S(2)}) copy-start(f32[128]{0:T(128)} %param.12) | copy-start | bytes 1540
  111.3 5.8 %collective-permute-start = (bf16[128,128]{0,1:T(8,128)(2,1)S(1)}, bf16[128,128]{0,1:T(8,128)(2,1)S(1)}, u32[]{:S(2)}, u32[]{:S(2)}) collective-permute-start(bf16[128,128]{0,1:T(8,128)(2,1)S(1)} %fusion.18), channel_id=1, source_target_pairs={{0,1},{1,0},{2,3},{3,2},{4,5},{5,4},{6,7},{7,6},{8,9},{9,8},{10,11... | collective-permute-start | bytes 98312 | tf_op jit(solution)/shard_map/ppermute | solution.py:15
  117.2 1.4 copy-start.4
  122.5 4.8 %copy-start.2 = (bf16[960,4,128]{2,0,1:T(8,128)(2,1)}, bf16[960,4,128]{2,0,1:T(8,128)(2,1)S(1)}, u32[]{:S(2)}) copy-start(bf16[960,4,128]{2,0,1:T(8,128)(2,1)S(1)} %fusion.8) | copy-start | bytes 2949124
  123.8 5.8 %collective-permute-start.1 = (bf16[128,128]{0,1:T(8,128)(2,1)S(1)}, bf16[128,128]{0,1:T(8,128)(2,1)S(1)}, u32[]{:S(2)}, u32[]{:S(2)}) collective-permute-start(bf16[128,128]{0,1:T(8,128)(2,1)S(1)} %pad_maximum_fusion.2), channel_id=1, source_target_pairs={{0,1},{1,0},{2,3},{3,2},{4,5},{5,4},{6,7},{7,6},{8,9},{9,8},{10,11... | collective-permute-start | bytes 98312 | tf_op jit(solution)/shard_map/ppermute | solution.py:15
  135.6 217.2 %reduce-scatter.7.cloned.1.call-start = ((), (), s32[]{:S(2)}) async-start(), calls=%async_computation.3 | async-start | bytes 2088960
Sparse Core Ops, SparseCore 0:
  11.9 97.0 all-gather.1
  135.7 127.2 reduce-scatter.8
  266.1 86.6 reduce-scatter.6
where the time goes:
time: 362 us; the launch traced here: 361 us
  waiting for transfers between devices  292 us (81%)
  local copies, waits for them, and re-layouts  24.8 us (7%)
  matrix products  16.3 us (5%)
  between operations  14.6 us (4%)
  starting transfers between devices  6.88 us (2%)
  other arithmetic  6.79 us (2%)
    unnamed x5, waiting for transfers between devices  194 us
    all_gather x1, waiting for transfers between devices, shards(): whole_weights = lax.all_gather(stacked, 'dp', axis=0, tiled=True)  92.7 us
    unnamed x20, local copies, waits for them, and re-layouts  21.1 us
  transfers between devices with their start and end apart: 5, of which 5 were waited for; matrix products, arithmetic and copies ran while one was open for 8% of the time, Pallas kernels for 0%

commit v1 on v0

v1 whole, which is shorter than its diff:
```python
import functools
import math

import jax
import jax.numpy as jnp
from jax import lax
from jax.experimental import pallas as pl
from jax.experimental.pallas import tpu as pltpu
from jax.sharding import PartitionSpec as P

TILE_ROWS = 32
EPS = 1e-05
HD = 128
Y, X, ZL = 8, 4, 4
CH = 160
HOPS = {(0, 0): 4, (0, 1): 3, (1, 0): 3, (1, 1): 4}
F32 = jnp.float32
BF16 = jnp.bfloat16
NT = (((1,), (1,)), ((), ()))
TN = (((0,), (0,)), ((), ()))


def dot(a, b, dims=(((1,), (0,)), ((), ()))):
    return lax.dot_general(a, b, dims, preferred_element_type=F32)


def kernel(
    tc_ref, q_hbm, feat_hbm, kwt_hbm, vwt_hbm, qg_hbm, kg_hbm, do_hbm,
    dq_hbm, ft_hbm, kgw_hbm, vgw_hbm,
    q_s, do_s, dq_s, feat_s, featT, wbuf, dsT, qn_s, w2_s, own_s, par_s, kbf_s, vbf_s, far_s,
    farr_s, g4_s, fterm, wterm, xr_s, yr_s, x1_s, x2_s, hz_s, hzr_s, vg_s, kg_s,
    kwt_s, vwt_s, qg_s, kg_in_s, ft_s, kgw_s, vgw_s,
    loc_sem, ag_ss, ag_rs, agz_ss, agz_rs, agc_ss, agc_rs, p_ss, p_rs,
    c_ss, c_rs, y_ss, y_rs, x_ss, x_rs, zf_ss, zf_rs, wc_ss, wc_rs, gz_ss, gz_rs, h_ss, h_rs,
):
    d = lax.axis_index("dp")
    t = lax.axis_index("tensor")
    y, zh, core = d // 4, (d // 2) % 2, d % 2
    zl, x = t // 4, t % 4
    low = (t % 2) == 0

    def at_y(step):
        return (((y + step + Y) % Y) * 4 + zh * 2 + core, t)

    right, left = at_y(1), at_y(-1)
    far_core = (d + 1 - 2 * core, t)
    far_z = (d + 2 - 4 * zh, t)
    partner = (d, t + 1 - 2 * (t % 2))
    x_right = (d, zl * 4 + (x + 1) % X)
    x_left = (d, zl * 4 + (x + X - 1) % X)
    z_to = [(d, ((zl + k) % ZL) * 4 + x) for k in (1, 2, 3)]

    barrier = pltpu.get_barrier_semaphore()
    peers = [right, left, far_core, far_z, x_right, x_left] + z_to
    for peer in peers:
        pl.semaphore_signal(barrier, inc=1, device_id=peer, device_id_type=pl.DeviceIdType.MESH)

    tokens = q_s.shape[0]
    heads = q_s.shape[1] // HD
    width = CH * heads
    fetched = (
        (kwt_hbm, kwt_s), (vwt_hbm, vwt_s), (feat_hbm, feat_s), (q_hbm, q_s), (do_hbm, do_s),
        (qg_hbm, qg_s), (kg_hbm, kg_in_s),
    )
    copies = [
        pltpu.make_async_copy(src, dst, loc_sem.at[i]) for i, (src, dst) in enumerate(fetched)
    ]
    for copy in copies:
        copy.start()

    sent = []

    def send(src, dst, ssem, rsem, dev):
        copy = pltpu.make_async_remote_copy(
            src_ref=src, dst_ref=dst, send_sem=ssem, recv_sem=rsem,
            device_id=dev, device_id_type=pl.DeviceIdType.MESH,
        )
        copy.start()
        sent.append(copy)
        return copy

    copies[0].wait()
    copies[1].wait()
    shard = jnp.concatenate((kwt_s[...], vwt_s[...]), 0).astype(F32)
    rows = shard.shape[1]
    shard = jnp.concatenate((shard, jnp.zeros((HD, 256 - rows), F32)), 1)
    mine = 2 * y + zh
    wbuf[mine, core] = jnp.transpose(shard)[:rows].astype(BF16)

    pl.semaphore_wait(barrier, len(peers))

    def c_of(step, stream):
        zz = zh if stream == 0 else 1 - zh
        return 2 * ((y + step + Y) % Y) + zz

    def gather_send(stream, way, hop):
        c = c_of((1 - hop) if way == 0 else (hop - 1), stream)
        ref = wbuf.at[c, core]
        return send(ref, ref, ag_ss.at[stream, way, hop - 1], ag_rs.at[stream, way, hop - 1],
                    right if way == 0 else left)

    across = []

    def core_send(c):
        ref = wbuf.at[c, core]
        i = len(across)
        across.append(send(ref, ref, agc_ss.at[i], agc_rs.at[i], far_core))

    def z_copy(c):
        dest = c // ZL
        return dest, pltpu.make_async_remote_copy(
            src_ref=wbuf.at[c, core], dst_ref=w2_s.at[zl, c % ZL, core],
            send_sem=zf_ss.at[c], recv_sem=zf_rs.at[zl, c % ZL],
            device_id=(d, dest * X + x), device_id_type=pl.DeviceIdType.MESH,
        )

    def z_send(c):
        dest, copy = z_copy(c)

        @pl.when(dest != zl)
        def _():
            copy.start()

    ag = {}
    for way in (0, 1):
        ag[0, way, 1] = gather_send(0, way, 1)
    ref = wbuf.at[mine, core]
    zcopy = send(ref, ref, agz_ss, agz_rs, far_z)
    core_send(mine)
    z_send(mine)

    copies[2].wait()
    copies[3].wait()
    copies[5].wait()
    copies[6].wait()
    inverse = 1.0 / math.sqrt(HD)
    qg = qg_s[...]
    kg = kg_in_s[...]

    def transpose_part(part):
        for i in range(part * 12, part * 12 + 12):
            featT[i * 128:(i + 1) * 128, :] = jnp.transpose(
                feat_s[:, i * 128:(i + 1) * 128].astype(F32)
            ).astype(BF16)

    def stack(ref, chunk):
        at = slice(chunk * CH, (chunk + 1) * CH)
        return jnp.concatenate([ref[at, h * HD:(h + 1) * HD] for h in range(heads)], 0)

    def query_norm(chunk):
        xq = stack(q_s, chunk).astype(F32)
        r = lax.rsqrt(jnp.mean(xq * xq, -1, keepdims=True) + EPS)
        qn_s[chunk * width:(chunk + 1) * width, :] = (xq * r * qg).astype(BF16)

    def gather_step(stream, hop):
        for way in (0, 1):
            if hop > HOPS[stream, way]:
                continue
            ag[stream, way, hop].wait_recv()
            if hop < HOPS[stream, way]:
                ag[stream, way, hop + 1] = gather_send(stream, way, hop + 1)
            c = c_of(-hop if way == 0 else hop, stream)
            core_send(c)
            z_send(c)

    for hop in range(1, 6):
        if hop <= 4:
            transpose_part(hop - 1)
            gather_step(0, hop)
        if hop == 1:
            zcopy.wait_recv()
            for way in (0, 1):
                ag[1, way, 1] = gather_send(1, way, 1)
            core_send(c_of(0, 1))
            z_send(c_of(0, 1))
        else:
            gather_step(1, hop - 1)
        query_norm(hop - 1)
    for copy in across:
        copy.wait_recv()

    proj = jnp.zeros((HD, HD), F32)
    for part in range(4):
        cols = feat_s[:, part * 1920:(part + 1) * 1920]
        proj += dot(cols, wbuf[part * 4:(part + 1) * 4].reshape(1920, HD))
    own_s[...] = proj.astype(BF16)
    pcopy = send(own_s, par_s, p_ss.at[0], p_rs.at[0], partner)
    copies[4].wait()
    transpose_part(4)
    query_norm(5)
    lane = lax.broadcasted_iota(jnp.int32, (HD, HD), 1)
    half = lane < 64
    lowf = jnp.where(low, 1.0, 0.0).astype(F32)
    own = own_s[...].astype(F32)
    pcopy.wait_recv()
    other = par_s[...].astype(F32)
    first = own * lowf + other * (1.0 - lowf)
    second = other * lowf + own * (1.0 - lowf)
    keys = jnp.where(half, first, pltpu.roll(second, 64, 1))
    values = jnp.where(half, pltpu.roll(first, 64, 1), second)
    k_scale = lax.rsqrt(jnp.mean(keys * keys, -1, keepdims=True) + EPS)
    kbf_s[...] = (keys * k_scale * kg).astype(BF16)
    vbf_s[...] = values.astype(BF16)
    live = (
        lax.broadcasted_iota(jnp.int32, (HD, 1), 0) < tc_ref[0] * TILE_ROWS
    ).astype(F32)
    vg_s[...] = jnp.zeros_like(vg_s)
    kg_s[...] = jnp.zeros_like(kg_s)

    def attend(chunk, carry):
        at = pl.ds(pl.multiple_of(chunk * CH, CH), CH)
        wide = pl.ds(pl.multiple_of(chunk * width, width), width)
        qn = qn_s[wide, :]
        do = jnp.concatenate([do_s[at, h * HD:(h + 1) * HD] for h in range(heads)], 0)
        e = jnp.exp(dot(kbf_s[...], qn, NT) * inverse) * live
        p = e * (1.0 / jnp.sum(e, 0, keepdims=True))
        pb = p.astype(BF16)
        vg_s[...] += dot(pb, do)
        pg = dot(vbf_s[...], do, NT)
        delta = jnp.sum(pb.astype(F32) * pg, 0, keepdims=True)
        ds = (p * (pg - delta)).astype(BF16)
        dsT[:, wide] = ds
        kg_s[...] += dot(ds, qn)
        return carry

    lax.fori_loop(0, tokens // CH, attend, 0, unroll=2)

    weighted = kg_s[...] * (inverse * kg)
    key_grad = k_scale * weighted - keys * (
        k_scale * k_scale * k_scale * jnp.mean(weighted * keys, -1, keepdims=True)
    )
    value_grad = vg_s[...]
    low_part = jnp.where(half, key_grad, pltpu.roll(value_grad, 64, 1))
    high_part = jnp.where(half, pltpu.roll(key_grad, 64, 1), value_grad)
    far_s[...] = (high_part * lowf + low_part * (1.0 - lowf)).astype(BF16)
    own_grad = low_part * lowf + high_part * (1.0 - lowf)
    fcopy = send(far_s, farr_s, p_ss.at[1], p_rs.at[1], partner)

    def query_back(chunk):
        xq = stack(q_s, chunk).astype(F32)
        r = lax.rsqrt(jnp.mean(xq * xq, -1, keepdims=True) + EPS)
        ds = dsT[:, chunk * width:(chunk + 1) * width]
        u = dot(ds, kbf_s[...], TN) * (inverse * qg)
        m = jnp.mean(u * xq, -1, keepdims=True)
        back = (r * u - xq * (r * r * r * m)).astype(BF16)
        for h in range(heads):
            dq_s[chunk * CH:(chunk + 1) * CH, h * HD:(h + 1) * HD] = back[h * CH:(h + 1) * CH]

    query_back(0)
    fcopy.wait_recv()
    g4_s[zl] = (own_grad + farr_s[...].astype(F32)).astype(BF16)
    g = g4_s[zl]
    gz = []
    for k in (1, 2, 0):
        gz.append(send(g4_s.at[zl], g4_s.at[zl], gz_ss.at[k], gz_rs.at[k], z_to[k]))

    order = (4, 3, 5, 2, 6, 1, 7, 0)
    crossing = {}
    for i, step in enumerate(order):
        yy = (y + step) % Y
        pair = featT[pl.ds(pl.multiple_of(yy * 960, 960), 960), :]
        wterm[pl.ds(2 * yy, 2)] = dot(pair, g).astype(BF16).reshape(2, 2, 240, HD)
        crossing[step] = send(
            wterm.at[pl.ds(2 * yy, 2), 1 - core], xr_s.at[pl.ds(2 * yy, 2)],
            c_ss.at[i], c_rs.at[i], far_core,
        )

    def feature_term(xx):
        total = dot(wbuf[zl * X + xx].reshape(480, HD), g, NT)
        for dz in (1, 2, 3):
            src = (zl + dz) % ZL
            total += dot(w2_s[src, xx].reshape(480, HD), g4_s[src], NT)
        return total

    x2, xp, xm = (x + 2) % X, (x + 1) % X, (x + 3) % X
    xs = {}

    def x_send(name, slot, src, dst, dev):
        xs[name] = send(src, dst, x_ss.at[slot], x_rs.at[slot], dev)

    def x_start():
        for copy in gz + wc:
            copy.wait_recv()
        for xx in (x2, xp, xm):
            fterm[xx] = feature_term(xx).astype(BF16).reshape(2, 240, HD)
            if xx is x2:
                x_send("r1", 0, fterm.at[x2, 0], x1_s.at[0], x_right)
                x_send("l1", 1, fterm.at[x2, 1], x1_s.at[1], x_left)
            elif xx is xp:
                x_send("r2", 2, fterm.at[xp, 1], x2_s.at[0, 1], x_right)
            else:
                x_send("l2", 3, fterm.at[xm, 0], x2_s.at[1, 0], x_left)

    wc = []

    def w2_across():
        for dz in (1, 3, 2):
            src = (zl + dz) % ZL
            for i in range(4):
                ref = w2_s.at[src, i, core]
                pltpu.make_async_remote_copy(
                    src_ref=ref, dst_ref=ref, send_sem=zf_ss.at[0], recv_sem=zf_rs.at[src, i],
                    device_id=far_core, device_id_type=pl.DeviceIdType.MESH,
                ).wait_recv()
                wc.append(send(ref, ref, wc_ss.at[dz - 1, i], wc_rs.at[dz - 1, i], far_core))

    slots = {}
    for key in ((0, 0), (1, 1), (0, 1), (1, 0)):
        for hop in range(1, HOPS[key] + 1):
            slots[key + (hop,)] = len(slots)
    ys = {}

    def merge(step, streams=(0, 1)):
        crossing[step % Y].wait_recv()
        for stream in streams:
            c = c_of(step, stream)
            total = wterm[c, core].astype(F32) + xr_s[c].astype(F32)
            wterm[c, core] = total.astype(BF16)

    def ring_send(stream, way, hop):
        step = HOPS[stream, way] - hop + 1
        c = c_of(step if way == 0 else -step, stream)
        slot = slots[stream, way, hop]
        if hop > 1:
            ys[stream, way, hop - 1].wait_recv()
            last = slots[stream, way, hop - 1]
            wterm[c, core] = (
                wterm[c, core].astype(F32) + yr_s[last].astype(F32)
            ).astype(BF16)
        ys[stream, way, hop] = send(
            wterm.at[c, core], yr_s.at[slot], y_ss.at[slot], y_rs.at[slot],
            right if way == 0 else left,
        )

    def x_relay():
        for name, way, xx in (("r", 0, xp), ("l", 1, xm)):
            xs[name + "1"].wait_recv()
            fterm[xx, way] = (
                fterm[xx, way].astype(F32) + x1_s[way].astype(F32)).astype(BF16)
            x_send(name + "3", 4 + way, fterm.at[xx, way], x2_s.at[way, way],
                   x_right if way == 0 else x_left)

    merge(4)
    ring_send(0, 0, 1)
    ring_send(1, 1, 1)
    merge(3)
    ring_send(1, 0, 1)
    merge(5)
    ring_send(0, 1, 1)
    w2_across()
    merge(2)
    merge(6)
    query_back(1)
    ring_send(0, 0, 2)
    ring_send(1, 1, 2)
    ring_send(1, 0, 2)
    ring_send(0, 1, 2)
    merge(1)
    merge(7)
    merge(0)
    x_start()
    ring_send(0, 0, 3)
    ring_send(1, 1, 3)
    ring_send(1, 0, 3)
    ring_send(0, 1, 3)
    own_term = feature_term(x)
    x_relay()
    query_back(2)
    query_back(3)
    ring_send(0, 0, 4)
    ring_send(1, 1, 4)
    for name in ("r2", "l2", "r3", "l3"):
        xs[name].wait_recv()
    own_term += x2_s[0].reshape(480, HD).astype(F32) + x2_s[1].reshape(480, HD).astype(F32)
    ft_s[...] = own_term.astype(BF16)
    query_back(4)
    query_back(5)
    outs = [
        pltpu.make_async_copy(dq_s, dq_hbm, loc_sem.at[7]),
        pltpu.make_async_copy(ft_s, ft_hbm, loc_sem.at[8]),
        pltpu.make_async_copy(kgw_s, kgw_hbm, loc_sem.at[9]),
        pltpu.make_async_copy(vgw_s, vgw_hbm, loc_sem.at[10]),
    ]
    outs[0].start()
    outs[1].start()

    def final_rows(stream):
        c = c_of(0, stream)
        total = wterm[c, core].astype(F32)
        for way in (0, 1):
            hop = HOPS[stream, way]
            ys[stream, way, hop].wait_recv()
            total += yr_s[slots[stream, way, hop]].astype(F32)
        return total

    hz_s[...] = final_rows(1).astype(BF16)
    hcopy = send(hz_s, hzr_s, h_ss, h_rs, far_z)
    own_rows = final_rows(0)
    hcopy.wait_recv()
    own_rows += hzr_s[...].astype(F32)
    padded = jnp.concatenate((own_rows, jnp.zeros((256 - rows, HD), F32)), 0)
    turned = jnp.transpose(padded)
    kgw_s[...] = turned[:64, :rows]
    vgw_s[...] = turned[64:, :rows]
    outs[2].start()
    outs[3].start()
    for dz in (1, 2, 3):
        for i in range(4):
            z_copy(4 * ((zl + dz) % ZL) + i)[1].wait_send()
    for copy in sent:
        copy.wait_send()
    for copy in outs:
        copy.wait()


def copy_out(a, b, c, e, a_out, b_out, c_out, e_out, sems):
    copies = [
        pltpu.make_async_copy(src, dst, sems.at[i])
        for i, (src, dst) in enumerate(((a, a_out), (b, b_out), (c, c_out), (e, e_out)))
    ]
    for copy in copies:
        copy.start()
    for copy in copies:
        copy.wait()


def shards(
    queries, features, key_weight, value_weight, query_gain, key_gain, out_grad, tile_counts
):
    samples, own_rows, feature_width = features.shape
    tokens, q_width = queries.shape
    rows, column_half = key_weight.shape
    anyspec = pl.BlockSpec(memory_space=pl.ANY)
    dma = pltpu.SemaphoreType.DMA
    piece = (rows, HD)
    scratch = [
        pltpu.VMEM((tokens, q_width), BF16),
        pltpu.VMEM((tokens, q_width), BF16),
        pltpu.VMEM((tokens, q_width), BF16),
        pltpu.VMEM((own_rows, feature_width), BF16),
        pltpu.VMEM((feature_width, own_rows), BF16),
        pltpu.VMEM((16, 2) + piece, BF16),
        pltpu.VMEM((HD, tokens * q_width // HD), BF16),
        pltpu.VMEM((tokens * q_width // HD, HD), BF16),
        pltpu.VMEM((ZL, X, 2) + piece, BF16),
    ]
    scratch += [pltpu.VMEM((HD, HD), BF16)] * 6
    scratch += [
        pltpu.VMEM((ZL, HD, HD), BF16),
        pltpu.VMEM((X, 2) + piece, BF16),
        pltpu.VMEM((16, 2) + piece, BF16),
        pltpu.VMEM((16,) + piece, BF16),
        pltpu.VMEM((14,) + piece, BF16),
        pltpu.VMEM((2,) + piece, BF16),
        pltpu.VMEM((2, 2) + piece, BF16),
        pltpu.VMEM(piece, BF16),
        pltpu.VMEM(piece, BF16),
        pltpu.VMEM((HD, HD), F32),
        pltpu.VMEM((HD, HD), F32),
        pltpu.VMEM((column_half, rows), BF16),
        pltpu.VMEM((column_half, rows), BF16),
        pltpu.VMEM((1, HD), F32),
        pltpu.VMEM((1, HD), F32),
        pltpu.VMEM((2 * rows, own_rows), BF16),
        pltpu.VMEM((column_half, rows), F32),
        pltpu.VMEM((column_half, rows), F32),
        dma((11,)),
        dma((2, 2, 4)), dma((2, 2, 4)), dma, dma, dma((16,)), dma((16,)), dma((2,)), dma((2,)),
        dma((8,)), dma((8,)), dma((14,)), dma((14,)), dma((6,)), dma((6,)),
        dma((16,)), dma((4, 4)), dma((3, 4)), dma((3, 4)), dma((3,)), dma((3,)), dma, dma,
    ]
    out_shape = (
        jax.ShapeDtypeStruct((tokens, q_width), BF16),
        jax.ShapeDtypeStruct((2 * rows, own_rows), BF16),
        jax.ShapeDtypeStruct((column_half, rows), F32),
        jax.ShapeDtypeStruct((column_half, rows), F32),
    )
    results = pl.pallas_call(
        kernel,
        out_shape=out_shape,
        in_specs=[pl.BlockSpec(memory_space=pltpu.SMEM)] + [anyspec] * 7,
        out_specs=(anyspec,) * 4,
        scratch_shapes=scratch,
        compiler_params=pltpu.CompilerParams(
            collective_id=0, has_side_effects=True, vmem_limit_bytes=62 * 1024 * 1024
        ),
        cost_estimate=pl.CostEstimate(
            flops=1600000000, bytes_accessed=8000000, transcendentals=500000
        ),
    )(
        tile_counts, queries, features.reshape(own_rows, feature_width), key_weight.T,
        value_weight.T, query_gain.reshape(1, HD), key_gain.reshape(1, HD), out_grad,
    )
    query_grad, feature_t, key_t, value_t = pl.pallas_call(
        copy_out,
        out_shape=out_shape,
        in_specs=[anyspec] * 4,
        out_specs=(anyspec,) * 4,
        scratch_shapes=[dma((4,))],
        compiler_params=pltpu.CompilerParams(vmem_limit_bytes=62 * 1024 * 1024),
        cost_estimate=pl.CostEstimate(flops=0, bytes_accessed=3000000, transcendentals=0),
    )(*results)
    return (query_grad, feature_t.T.reshape(samples, own_rows, 2 * rows), key_t.T, value_t.T)


def solution(mesh):
    placed = (
        P("dp", "tensor"),
        P("dp", None, None),
        P("dp", "tensor"),
        P("dp", "tensor"),
        P(),
        P(),
        P("dp", "tensor"),
        P("dp"),
    )
    return jax.shard_map(
        shards,
        mesh=mesh,
        in_specs=placed,
        out_specs=(
            P("dp", "tensor"),
            P("dp", None, "tensor"),
            P("dp", "tensor"),
            P("dp", "tensor"),
        ),
        check_vma=False,
    )
```

time: 362 us -> 112 us (0.31)
  the two profiles are of different devices: /device:TPU:8 before, /device:TPU:136 now
where the time goes in v1:
time: 112 us
  Pallas kernels  111 us (99%)
  between operations  1.29 us (1%)
    pallas_call x1, Pallas kernels, shards(): pl.pallas_call(kernel, out_shape=out_shape, in_specs=[pl.BlockSpec(memory...  72 us
    pallas_call x1, Pallas kernels, shards(): pl.pallas_call(copy_out, out_shape=out_shape, in_specs=[anyspec] * 4, out...  38.6 us

profile of v1, /device:TPU:136, one launch (start us, length us, event | category | flops | bytes accessed | tf_op | source)
XLA Modules:
  0.0 111.9 jit_solution(280871021660266884)
XLA Ops:
  1.3 72.0 %shard_map.111 = (bf16[960,512]{1,0:T(8,128)(2,1)}, bf16[480,128]{1,0:T(8,128)(2,1)}, f32[64,240]{1,0:T(8,128)}, f32[64,240]{1,0:T(8,128)}) custom-call(s32[1]{0:T(128)S(6)} %copy.12.tc_ref, bf16[960,512]{1,0:T(8,128)(2,1)} %q_hbm.1, bf16[128,7680]{1,0:T(8,128)(2,1)} %bitcast.10, bf16[64,240]{1,0:T(8,128)(2,1)} %bitcast.14, bf16[64,240]{1,0:T(8,128)(2,1)} %bitcast.15, ...), custom_call_target="tpu_custom_call" | custom-call | flops 1600000000 | bytes 8000000 | tf_op jit(solution)/shard_map/pallas_call | solution.py:478
  73.3 38.6 %shard_map.112 = (bf16[960,512]{1,0:T(8,128)(2,1)}, bf16[480,128]{1,0:T(8,128)(2,1)}, f32[64,240]{1,0:T(8,128)}, f32[64,240]{1,0:T(8,128)}) custom-call(bf16[960,512]{1,0:T(8,128)(2,1)} %get-tuple-element.12.a, bf16[480,128]{1,0:T(8,128)(2,1)} %get-tuple-element.13.b, f32[64,240]{1,0:T(8,128)} %get-tuple-element.14.c, f32[64,240]{1,0:T(8,128)} %get-tuple-element.15.e), custom_call_target="tpu_custom_call" | custom-call | bytes 3000000 | tf_op jit(solution)/shard_map/pallas_call | solution.py:494

commit v2 on v1

--- a/solution.py
+++ b/solution.py
@@ -28,7 +28,7 @@
     tc_ref, q_hbm, feat_hbm, kwt_hbm, vwt_hbm, qg_hbm, kg_hbm, do_hbm,
     dq_hbm, ft_hbm, kgw_hbm, vgw_hbm,
     q_s, do_s, dq_s, feat_s, featT, wbuf, dsT, qn_s, w2_s, own_s, par_s, kbf_s, vbf_s, far_s,
-    farr_s, g4_s, fterm, wterm, xr_s, yr_s, x1_s, x2_s, hz_s, hzr_s, vg_s, kg_s,
+    farr_s, g4_s, go_s, fterm, wterm, fx_s, yr_s, x1_s, x2_s, hz_s, hzr_s, vg_s, kg_s,
     kwt_s, vwt_s, qg_s, kg_in_s, ft_s, kgw_s, vgw_s,
     loc_sem, ag_ss, ag_rs, agz_ss, agz_rs, agc_ss, agc_rs, p_ss, p_rs,
     c_ss, c_rs, y_ss, y_rs, x_ss, x_rs, zf_ss, zf_rs, wc_ss, wc_rs, gz_ss, gz_rs, h_ss, h_rs,
@@ -137,11 +137,14 @@
     qg = qg_s[...]
     kg = kg_in_s[...]
 
+    shared = []
+
     def transpose_part(part):
-        for i in range(part * 12, part * 12 + 12):
-            featT[i * 128:(i + 1) * 128, :] = jnp.transpose(
-                feat_s[:, i * 128:(i + 1) * 128].astype(F32)
-            ).astype(BF16)
+        cols = feat_s[:, part * 1920:(part + 1) * 1920]
+        group = pl.ds(part * 4, 4)
+        featT[group] = jnp.transpose(cols).reshape(4, 2, 240, HD)
+        shared.append(send(
+            featT.at[group, 1 - core], fx_s.at[group], c_ss.at[part], c_rs.at[part], far_core))
 
     def stack(ref, chunk):
         at = slice(chunk * CH, (chunk + 1) * CH)
@@ -163,6 +166,17 @@
             core_send(c)
             z_send(c)
 
+    arrived = 0
+
+    def project(parts):
+        total = jnp.zeros((HD, HD), F32)
+        for part in parts:
+            at = (y // 2 + part) % 4
+            cols = feat_s[:, pl.ds(pl.multiple_of(at * 1920, 1920), 1920)]
+            total += dot(cols, wbuf[pl.ds(4 * at, 4)].reshape(1920, HD))
+        return total
+
+    proj = jnp.zeros((HD, HD), F32)
     for hop in range(1, 6):
         if hop <= 4:
             transpose_part(hop - 1)
@@ -175,18 +189,18 @@
             z_send(c_of(0, 1))
         else:
             gather_step(1, hop - 1)
-        query_norm(hop - 1)
-    for copy in across:
-        copy.wait_recv()
-
-    proj = jnp.zeros((HD, HD), F32)
-    for part in range(4):
-        cols = feat_s[:, part * 1920:(part + 1) * 1920]
-        proj += dot(cols, wbuf[part * 4:(part + 1) * 4].reshape(1920, HD))
+        if hop <= 4:
+            query_norm(hop - 1)
+        if hop >= 3:
+            until, parts = {3: (8, (0,)), 4: (15, (1, 3)), 5: (16, (2,))}[hop]
+            for copy in across[arrived:until]:
+                copy.wait_recv()
+            arrived = until
+            proj += project(parts)
     own_s[...] = proj.astype(BF16)
     pcopy = send(own_s, par_s, p_ss.at[0], p_rs.at[0], partner)
     copies[4].wait()
-    transpose_part(4)
+    query_norm(4)
     query_norm(5)
     lane = lax.broadcasted_iota(jnp.int32, (HD, HD), 1)
     half = lane < 64
@@ -223,7 +237,7 @@
         kg_s[...] += dot(ds, qn)
         return carry
 
-    lax.fori_loop(0, tokens // CH, attend, 0, unroll=2)
+    lax.fori_loop(0, tokens // CH, attend, 0, unroll=3)
 
     weighted = kg_s[...] * (inverse * kg)
     key_grad = k_scale * weighted - keys * (
@@ -250,20 +264,21 @@
     fcopy.wait_recv()
     g4_s[zl] = (own_grad + farr_s[...].astype(F32)).astype(BF16)
     g = g4_s[zl]
+    gcopy = send(g4_s.at[zl], go_s, c_ss.at[4], c_rs.at[4], far_core)
     gz = []
     for k in (1, 2, 0):
         gz.append(send(g4_s.at[zl], g4_s.at[zl], gz_ss.at[k], gz_rs.at[k], z_to[k]))
 
-    order = (4, 3, 5, 2, 6, 1, 7, 0)
-    crossing = {}
-    for i, step in enumerate(order):
-        yy = (y + step) % Y
-        pair = featT[pl.ds(pl.multiple_of(yy * 960, 960), 960), :]
-        wterm[pl.ds(2 * yy, 2)] = dot(pair, g).astype(BF16).reshape(2, 2, 240, HD)
-        crossing[step] = send(
-            wterm.at[pl.ds(2 * yy, 2), 1 - core], xr_s.at[pl.ds(2 * yy, 2)],
-            c_ss.at[i], c_rs.at[i], far_core,
-        )
+    query_back(1)
+    gcopy.wait_recv()
+    go = go_s[...]
+    for copy in shared:
+        copy.wait_recv()
+
+    def weight_term(step):
+        for stream in (1, 0):
+            c = c_of(step, stream)
+            wterm[c] = (dot(featT[c, core], g) + dot(fx_s[c], go)).astype(BF16)
 
     def feature_term(xx):
         total = dot(wbuf[zl * X + xx].reshape(480, HD), g, NT)
@@ -310,13 +325,6 @@
             slots[key + (hop,)] = len(slots)
     ys = {}
 
-    def merge(step, streams=(0, 1)):
-        crossing[step % Y].wait_recv()
-        for stream in streams:
-            c = c_of(step, stream)
-            total = wterm[c, core].astype(F32) + xr_s[c].astype(F32)
-            wterm[c, core] = total.astype(BF16)
-
     def ring_send(stream, way, hop):
         step = HOPS[stream, way] - hop + 1
         c = c_of(step if way == 0 else -step, stream)
@@ -324,11 +332,9 @@
         if hop > 1:
             ys[stream, way, hop - 1].wait_recv()
             last = slots[stream, way, hop - 1]
-            wterm[c, core] = (
-                wterm[c, core].astype(F32) + yr_s[last].astype(F32)
-            ).astype(BF16)
+            wterm[c] = (wterm[c].astype(F32) + yr_s[last].astype(F32)).astype(BF16)
         ys[stream, way, hop] = send(
-            wterm.at[c, core], yr_s.at[slot], y_ss.at[slot], y_rs.at[slot],
+            wterm.at[c], yr_s.at[slot], y_ss.at[slot], y_rs.at[slot],
             right if way == 0 else left,
         )
 
@@ -340,35 +346,32 @@
             x_send(name + "3", 4 + way, fterm.at[xx, way], x2_s.at[way, way],
                    x_right if way == 0 else x_left)
 
-    merge(4)
+    def ring_hop(hop):
+        for stream, way in ((1, 1), (1, 0), (0, 0), (0, 1)):
+            if hop <= HOPS[stream, way]:
+                ring_send(stream, way, hop)
+
+    weight_term(4)
+    ring_send(1, 1, 1)
     ring_send(0, 0, 1)
-    ring_send(1, 1, 1)
-    merge(3)
+    weight_term(3)
     ring_send(1, 0, 1)
-    merge(5)
+    weight_term(5)
     ring_send(0, 1, 1)
+    weight_term(2)
+    weight_term(6)
     w2_across()
-    merge(2)
-    merge(6)
-    query_back(1)
-    ring_send(0, 0, 2)
-    ring_send(1, 1, 2)
-    ring_send(1, 0, 2)
-    ring_send(0, 1, 2)
-    merge(1)
-    merge(7)
-    merge(0)
+    ring_hop(2)
+    weight_term(1)
+    weight_term(7)
+    weight_term(0)
     x_start()
-    ring_send(0, 0, 3)
-    ring_send(1, 1, 3)
-    ring_send(1, 0, 3)
-    ring_send(0, 1, 3)
+    ring_hop(3)
     own_term = feature_term(x)
     x_relay()
     query_back(2)
     query_back(3)
-    ring_send(0, 0, 4)
-    ring_send(1, 1, 4)
+    ring_hop(4)
     for name in ("r2", "l2", "r3", "l3"):
         xs[name].wait_recv()
     own_term += x2_s[0].reshape(480, HD).astype(F32) + x2_s[1].reshape(480, HD).astype(F32)
@@ -386,7 +389,7 @@
 
     def final_rows(stream):
         c = c_of(0, stream)
-        total = wterm[c, core].astype(F32)
+        total = wterm[c].astype(F32)
         for way in (0, 1):
             hop = HOPS[stream, way]
             ys[stream, way, hop].wait_recv()
@@ -413,14 +416,24 @@
         copy.wait()
 
 
-def copy_out(a, b, c, e, a_out, b_out, c_out, e_out, sems):
-    copies = [
-        pltpu.make_async_copy(src, dst, sems.at[i])
-        for i, (src, dst) in enumerate(((a, a_out), (b, b_out), (c, c_out), (e, e_out)))
+def copy_out(a, b, c, e, a_out, b_out, c_out, e_out, a_s, b_s, c_s, e_s, in_sems, out_sems):
+    refs = [(b, b_s, b_out), (c, c_s, c_out), (e, e_s, e_out)]
+    step = a_s.shape[0] // 4
+    for i in range(4):
+        at = pl.ds(i * step, step)
+        refs.append((a.at[at], a_s.at[at], a_out.at[at]))
+    loads = [
+        pltpu.make_async_copy(src, mid, in_sems.at[i]) for i, (src, mid, dst) in enumerate(refs)
     ]
-    for copy in copies:
+    stores = [
+        pltpu.make_async_copy(mid, dst, out_sems.at[i]) for i, (src, mid, dst) in enumerate(refs)
+    ]
+    for copy in loads:
         copy.start()
-    for copy in copies:
+    for load, store in zip(loads, stores):
+        load.wait()
+        store.start()
+    for copy in stores:
         copy.wait()
 
 
@@ -438,7 +451,7 @@
         pltpu.VMEM((tokens, q_width), BF16),
         pltpu.VMEM((tokens, q_width), BF16),
         pltpu.VMEM((own_rows, feature_width), BF16),
-        pltpu.VMEM((feature_width, own_rows), BF16),
+        pltpu.VMEM((16, 2) + piece, BF16),
         pltpu.VMEM((16, 2) + piece, BF16),
         pltpu.VMEM((HD, tokens * q_width // HD), BF16),
         pltpu.VMEM((tokens * q_width // HD, HD), BF16),
@@ -447,8 +460,9 @@
     scratch += [pltpu.VMEM((HD, HD), BF16)] * 6
     scratch += [
         pltpu.VMEM((ZL, HD, HD), BF16),
+        pltpu.VMEM((HD, HD), BF16),
         pltpu.VMEM((X, 2) + piece, BF16),
-        pltpu.VMEM((16, 2) + piece, BF16),
+        pltpu.VMEM((16,) + piece, BF16),
         pltpu.VMEM((16,) + piece, BF16),
         pltpu.VMEM((14,) + piece, BF16),
         pltpu.VMEM((2,) + piece, BF16),
@@ -496,7 +510,7 @@
         out_shape=out_shape,
         in_specs=[anyspec] * 4,
         out_specs=(anyspec,) * 4,
-        scratch_shapes=[dma((4,))],
+        scratch_shapes=[pltpu.VMEM(o.shape, o.dtype) for o in out_shape] + [dma((7,)), dma((7,))],
         compiler_params=pltpu.CompilerParams(vmem_limit_bytes=62 * 1024 * 1024),
         cost_estimate=pl.CostEstimate(flops=0, bytes_accessed=3000000, transcendentals=0),
     )(*results)

time: 112 us -> 74.5 us (0.67)
  the two profiles are of different devices: /device:TPU:136 before, /device:TPU:128 now
where the time goes in v2:
time: 74.5 us; the launch traced here: 74.4 us
  Pallas kernels  73.1 us (98%)
  between operations  1.29 us (2%)
    pallas_call x1, Pallas kernels, shards(): pl.pallas_call(kernel, out_shape=out_shape, in_specs=[pl.BlockSpec(memory...  70.9 us
    pallas_call x1, Pallas kernels, shards(): pl.pallas_call(copy_out, out_shape=out_shape, in_specs=[anyspec] * 4, out...  2.21 us

profile of v2, /device:TPU:128, one launch (start us, length us, event | category | flops | bytes accessed | tf_op | source)
XLA Modules:
  0.0 74.4 jit_solution(10727622751416536831)
XLA Ops:
  1.3 70.9 %shard_map.111 = (bf16[960,512]{1,0:T(8,128)(2,1)}, bf16[480,128]{1,0:T(8,128)(2,1)}, f32[64,240]{1,0:T(8,128)}, f32[64,240]{1,0:T(8,128)}) custom-call(s32[1]{0:T(128)S(6)} %copy.12.tc_ref, bf16[960,512]{1,0:T(8,128)(2,1)} %q_hbm.1, bf16[128,7680]{1,0:T(8,128)(2,1)} %bitcast.10, bf16[64,240]{1,0:T(8,128)(2,1)} %bitcast.14, bf16[64,240]{1,0:T(8,128)(2,1)} %bitcast.15, ...), custom_call_target="tpu_custom_call" | custom-call | flops 1600000000 | bytes 8000000 | tf_op jit(solution)/shard_map/pallas_call | solution.py:492
  72.2 2.2 %shard_map.112 = (bf16[960,512]{1,0:T(8,128)(2,1)}, bf16[480,128]{1,0:T(8,128)(2,1)}, f32[64,240]{1,0:T(8,128)}, f32[64,240]{1,0:T(8,128)}) custom-call(bf16[960,512]{1,0:T(8,128)(2,1)} %get-tuple-element.12.a, bf16[480,128]{1,0:T(8,128)(2,1)} %get-tuple-element.13.b, f32[64,240]{1,0:T(8,128)} %get-tuple-element.14.c, f32[64,240]{1,0:T(8,128)} %get-tuple-element.15.e), custom_call_target="tpu_custom_call" | custom-call | bytes 3000000 | tf_op jit(solution)/shard_map/pallas_call | solution.py:508

commit v3 on v2

--- a/solution.py
+++ b/solution.py
@@ -31,13 +31,14 @@
     farr_s, g4_s, go_s, fterm, wterm, fx_s, yr_s, x1_s, x2_s, hz_s, hzr_s, vg_s, kg_s,
     kwt_s, vwt_s, qg_s, kg_in_s, ft_s, kgw_s, vgw_s,
     loc_sem, ag_ss, ag_rs, agz_ss, agz_rs, agc_ss, agc_rs, p_ss, p_rs,
-    c_ss, c_rs, y_ss, y_rs, x_ss, x_rs, zf_ss, zf_rs, wc_ss, wc_rs, gz_ss, gz_rs, h_ss, h_rs,
+    c_ss, c_rs, y_ss, y_rs, x_ss, x_rs, zf_ss, zf_rs, wc_ss, wc_rs, yp_ss, yp_rs, gz_ss, gz_rs, h_ss, h_rs,
 ):
     d = lax.axis_index("dp")
     t = lax.axis_index("tensor")
     y, zh, core = d // 4, (d // 2) % 2, d % 2
     zl, x = t // 4, t % 4
     low = (t % 2) == 0
+    par = y % 2
 
     def at_y(step):
         return (((y + step + Y) % Y) * 4 + zh * 2 + core, t)
@@ -45,6 +46,7 @@
     right, left = at_y(1), at_y(-1)
     far_core = (d + 1 - 2 * core, t)
     far_z = (d + 2 - 4 * zh, t)
+    y_pair = (d + 4 - 8 * par, t)
     partner = (d, t + 1 - 2 * (t % 2))
     x_right = (d, zl * 4 + (x + 1) % X)
     x_left = (d, zl * 4 + (x + X - 1) % X)
@@ -117,7 +119,7 @@
     def z_send(c):
         dest, copy = z_copy(c)
 
-        @pl.when(dest != zl)
+        @pl.when((dest != zl) & (c % 2 == par))
         def _():
             copy.start()
 
@@ -179,8 +181,8 @@
     proj = jnp.zeros((HD, HD), F32)
     for hop in range(1, 6):
         if hop <= 4:
+            gather_step(0, hop)
             transpose_part(hop - 1)
-            gather_step(0, hop)
         if hop == 1:
             zcopy.wait_recv()
             for way in (0, 1):
@@ -237,7 +239,34 @@
         kg_s[...] += dot(ds, qn)
         return carry
 
-    lax.fori_loop(0, tokens // CH, attend, 0, unroll=3)
+    swaps = []
+    wc = []
+    z_from = [(dz, j, (zl + dz) % ZL) for dz in (1, 3, 2) for j in (0, 1)]
+
+    def w2_send(src, i, dev, ssem, rsem):
+        ref = w2_s.at[src, i, core]
+        return send(ref, ref, ssem, rsem, dev)
+
+    def swap_pairs():
+        for dz, j, src in z_from:
+            i = 2 * j + par
+            ref = w2_s.at[src, i, core]
+            pltpu.make_async_remote_copy(
+                src_ref=ref, dst_ref=ref, send_sem=zf_ss.at[0], recv_sem=zf_rs.at[src, i],
+                device_id=far_core, device_id_type=pl.DeviceIdType.MESH,
+            ).wait_recv()
+            swaps.append(w2_send(src, i, y_pair, yp_ss.at[dz - 1, j], yp_rs.at[dz - 1, j]))
+            wc.append(w2_send(src, i, far_core, wc_ss.at[dz - 1, j], wc_rs.at[dz - 1, j]))
+
+    def swapped_across():
+        for (dz, j, src), copy in zip(z_from, swaps):
+            copy.wait_recv()
+            wc.append(w2_send(
+                src, 2 * j + 1 - par, far_core, wc_ss.at[dz - 1, 2 + j], wc_rs.at[dz - 1, 2 + j]))
+
+    lax.fori_loop(0, 2, attend, 0, unroll=2)
+    swap_pairs()
+    lax.fori_loop(2, tokens // CH, attend, 0, unroll=2)
 
     weighted = kg_s[...] * (inverse * kg)
     key_grad = k_scale * weighted - keys * (
@@ -306,19 +335,6 @@
             else:
                 x_send("l2", 3, fterm.at[xm, 0], x2_s.at[1, 0], x_left)
 
-    wc = []
-
-    def w2_across():
-        for dz in (1, 3, 2):
-            src = (zl + dz) % ZL
-            for i in range(4):
-                ref = w2_s.at[src, i, core]
-                pltpu.make_async_remote_copy(
-                    src_ref=ref, dst_ref=ref, send_sem=zf_ss.at[0], recv_sem=zf_rs.at[src, i],
-                    device_id=far_core, device_id_type=pl.DeviceIdType.MESH,
-                ).wait_recv()
-                wc.append(send(ref, ref, wc_ss.at[dz - 1, i], wc_rs.at[dz - 1, i], far_core))
-
     slots = {}
     for key in ((0, 0), (1, 1), (0, 1), (1, 0)):
         for hop in range(1, HOPS[key] + 1):
@@ -360,18 +376,18 @@
     ring_send(0, 1, 1)
     weight_term(2)
     weight_term(6)
-    w2_across()
-    ring_hop(2)
     weight_term(1)
     weight_term(7)
     weight_term(0)
+    ring_hop(2)
+    swapped_across()
+    query_back(2)
+    ring_hop(3)
     x_start()
-    ring_hop(3)
     own_term = feature_term(x)
+    ring_hop(4)
     x_relay()
-    query_back(2)
     query_back(3)
-    ring_hop(4)
     for name in ("r2", "l2", "r3", "l3"):
         xs[name].wait_recv()
     own_term += x2_s[0].reshape(480, HD).astype(F32) + x2_s[1].reshape(480, HD).astype(F32)
@@ -407,9 +423,8 @@
     vgw_s[...] = turned[64:, :rows]
     outs[2].start()
     outs[3].start()
-    for dz in (1, 2, 3):
-        for i in range(4):
-            z_copy(4 * ((zl + dz) % ZL) + i)[1].wait_send()
+    for dz, j, dest in z_from:
+        z_copy(4 * dest + 2 * j + par)[1].wait_send()
     for copy in sent:
         copy.wait_send()
     for copy in outs:
@@ -481,7 +496,7 @@
         dma((11,)),
         dma((2, 2, 4)), dma((2, 2, 4)), dma, dma, dma((16,)), dma((16,)), dma((2,)), dma((2,)),
         dma((8,)), dma((8,)), dma((14,)), dma((14,)), dma((6,)), dma((6,)),
-        dma((16,)), dma((4, 4)), dma((3, 4)), dma((3, 4)), dma((3,)), dma((3,)), dma, dma,
+        dma((16,)), dma((4, 4)), dma((3, 4)), dma((3, 4)), dma((3, 2)), dma((3, 2)), dma((3,)), dma((3,)), dma, dma,
     ]
     out_shape = (
         jax.ShapeDtypeStruct((tokens, q_width), BF16),

time: 74.5 us -> 76.9 us (1.032)
  the two profiles are of different devices: /device:TPU:128 before, /device:TPU:2 now
where the time goes in v3:
time: 76.9 us; the launch traced here: 76.8 us
  Pallas kernels  75.5 us (98%)
  between operations  1.29 us (2%)
    pallas_call x1, Pallas kernels, shards(): pl.pallas_call(kernel, out_shape=out_shape, in_specs=[pl.BlockSpec(memory...  73.3 us
    pallas_call x1, Pallas kernels, shards(): pl.pallas_call(copy_out, out_shape=out_shape, in_specs=[anyspec] * 4, out...  2.21 us

profile of v3, /device:TPU:2, one launch (start us, length us, event | category | flops | bytes accessed | tf_op | source)
XLA Modules:
  0.0 76.8 jit_solution(4390487767938409439)
XLA Ops:
  1.3 73.3 %shard_map.111 = (bf16[960,512]{1,0:T(8,128)(2,1)}, bf16[480,128]{1,0:T(8,128)(2,1)}, f32[64,240]{1,0:T(8,128)}, f32[64,240]{1,0:T(8,128)}) custom-call(s32[1]{0:T(128)S(6)} %copy.12.tc_ref, bf16[960,512]{1,0:T(8,128)(2,1)} %q_hbm.1, bf16[128,7680]{1,0:T(8,128)(2,1)} %bitcast.10, bf16[64,240]{1,0:T(8,128)(2,1)} %bitcast.14, bf16[64,240]{1,0:T(8,128)(2,1)} %bitcast.15, ...), custom_call_target="tpu_custom_call" | custom-call | flops 1600000000 | bytes 8000000 | tf_op jit(solution)/shard_map/pallas_call | solution.py:507
  74.6 2.2 %shard_map.112 = (bf16[960,512]{1,0:T(8,128)(2,1)}, bf16[480,128]{1,0:T(8,128)(2,1)}, f32[64,240]{1,0:T(8,128)}, f32[64,240]{1,0:T(8,128)}) custom-call(bf16[960,512]{1,0:T(8,128)(2,1)} %get-tuple-element.12.a, bf16[480,128]{1,0:T(8,128)(2,1)} %get-tuple-element.13.b, f32[64,240]{1,0:T(8,128)} %get-tuple-element.14.c, f32[64,240]{1,0:T(8,128)} %get-tuple-element.15.e), custom_call_target="tpu_custom_call" | custom-call | bytes 3000000 | tf_op jit(solution)/shard_map/pallas_call | solution.py:523

commit v4 on v2

--- a/solution.py
+++ b/solution.py
@@ -14,6 +14,7 @@
 Y, X, ZL = 8, 4, 4
 CH = 160
 HOPS = {(0, 0): 4, (0, 1): 3, (1, 0): 3, (1, 1): 4}
+PIECES = ((0, 240), (0, 128), (128, 112))
 F32 = jnp.float32
 BF16 = jnp.bfloat16
 NT = (((1,), (1,)), ((), ()))
@@ -28,7 +29,7 @@
     tc_ref, q_hbm, feat_hbm, kwt_hbm, vwt_hbm, qg_hbm, kg_hbm, do_hbm,
     dq_hbm, ft_hbm, kgw_hbm, vgw_hbm,
     q_s, do_s, dq_s, feat_s, featT, wbuf, dsT, qn_s, w2_s, own_s, par_s, kbf_s, vbf_s, far_s,
-    farr_s, g4_s, go_s, fterm, wterm, fx_s, yr_s, x1_s, x2_s, hz_s, hzr_s, vg_s, kg_s,
+    farr_s, g4_s, own_grad_s, other_grad_s, fterm, wterm, fx_s, yr_s, x1_s, x2_s, hz_s, hzr_s, vg_s, kg_s,
     kwt_s, vwt_s, qg_s, kg_in_s, ft_s, kgw_s, vgw_s,
     loc_sem, ag_ss, ag_rs, agz_ss, agz_rs, agc_ss, agc_rs, p_ss, p_rs,
     c_ss, c_rs, y_ss, y_rs, x_ss, x_rs, zf_ss, zf_rs, wc_ss, wc_rs, gz_ss, gz_rs, h_ss, h_rs,
@@ -46,18 +47,20 @@
     far_core = (d + 1 - 2 * core, t)
     far_z = (d + 2 - 4 * zh, t)
     partner = (d, t + 1 - 2 * (t % 2))
+    diagonal = (d + 1 - 2 * core, t + 1 - 2 * (t % 2))
     x_right = (d, zl * 4 + (x + 1) % X)
     x_left = (d, zl * 4 + (x + X - 1) % X)
     z_to = [(d, ((zl + k) % ZL) * 4 + x) for k in (1, 2, 3)]
 
     barrier = pltpu.get_barrier_semaphore()
-    peers = [right, left, far_core, far_z, x_right, x_left] + z_to
+    peers = [right, left, far_core, far_z, x_right, x_left, diagonal] + z_to
     for peer in peers:
         pl.semaphore_signal(barrier, inc=1, device_id=peer, device_id_type=pl.DeviceIdType.MESH)
 
     tokens = q_s.shape[0]
     heads = q_s.shape[1] // HD
     width = CH * heads
+    chunks = tokens // CH
     fetched = (
         (kwt_hbm, kwt_s), (vwt_hbm, vwt_s), (feat_hbm, feat_s), (q_hbm, q_s), (do_hbm, do_s),
         (qg_hbm, qg_s), (kg_hbm, kg_in_s),
@@ -70,6 +73,13 @@
 
     sent = []
 
+    def drain(later=()):
+        kept = [copy for copy in sent if any(copy is one for one in later)]
+        for copy in sent:
+            if not any(copy is one for one in later):
+                copy.wait_send()
+        sent[:] = kept
+
     def send(src, dst, ssem, rsem, dev):
         copy = pltpu.make_async_remote_copy(
             src_ref=src, dst_ref=dst, send_sem=ssem, recv_sem=rsem,
@@ -93,16 +103,19 @@
         zz = zh if stream == 0 else 1 - zh
         return 2 * ((y + step + Y) % Y) + zz
 
-    def gather_send(stream, way, hop):
-        c = c_of((1 - hop) if way == 0 else (hop - 1), stream)
-        ref = wbuf.at[c, core]
-        return send(ref, ref, ag_ss.at[stream, way, hop - 1], ag_rs.at[stream, way, hop - 1],
+    def piece_of(c, part):
+        return wbuf.at[c, core, pl.ds(*PIECES[part])]
+
+    def gather_send(part, way, hop):
+        c = c_of((1 - hop) if way == 0 else (hop - 1), min(part, 1))
+        ref = piece_of(c, part)
+        return send(ref, ref, ag_ss.at[part, way, hop - 1], ag_rs.at[part, way, hop - 1],
                     right if way == 0 else left)
 
     across = []
 
-    def core_send(c):
-        ref = wbuf.at[c, core]
+    def core_send(c, part):
+        ref = piece_of(c, part)
         i = len(across)
         across.append(send(ref, ref, agc_ss.at[i], agc_rs.at[i], far_core))
 
@@ -124,9 +137,11 @@
     ag = {}
     for way in (0, 1):
         ag[0, way, 1] = gather_send(0, way, 1)
-    ref = wbuf.at[mine, core]
-    zcopy = send(ref, ref, agz_ss, agz_rs, far_z)
-    core_send(mine)
+    zcopies = {}
+    for part in (1, 2):
+        ref = piece_of(mine, part)
+        zcopies[part] = send(ref, ref, agz_ss.at[part - 1], agz_rs.at[part - 1], far_z)
+    core_send(mine, 0)
     z_send(mine)
 
     copies[2].wait()
@@ -137,71 +152,77 @@
     qg = qg_s[...]
     kg = kg_in_s[...]
 
-    shared = []
-
-    def transpose_part(part):
-        cols = feat_s[:, part * 1920:(part + 1) * 1920]
+    def shared_copy(part):
         group = pl.ds(part * 4, 4)
-        featT[group] = jnp.transpose(cols).reshape(4, 2, 240, HD)
-        shared.append(send(
-            featT.at[group, 1 - core], fx_s.at[group], c_ss.at[part], c_rs.at[part], far_core))
+        return pltpu.make_async_remote_copy(
+            src_ref=featT.at[group, 1 - core], dst_ref=fx_s.at[group],
+            send_sem=c_ss.at[part], recv_sem=c_rs.at[part],
+            device_id=far_core, device_id_type=pl.DeviceIdType.MESH,
+        )
+
+    def transpose_part(part, carry):
+        cols = feat_s[:, pl.ds(pl.multiple_of(part * 1920, 1920), 1920)]
+        featT[pl.ds(part * 4, 4)] = jnp.transpose(cols).reshape(4, 2, 240, HD)
+        shared_copy(part).start()
+        return carry
 
     def stack(ref, chunk):
-        at = slice(chunk * CH, (chunk + 1) * CH)
+        at = pl.ds(pl.multiple_of(chunk * CH, CH), CH)
         return jnp.concatenate([ref[at, h * HD:(h + 1) * HD] for h in range(heads)], 0)
 
-    def query_norm(chunk):
+    def wide(chunk):
+        return pl.ds(pl.multiple_of(chunk * width, width), width)
+
+    def query_norm(chunk, carry):
         xq = stack(q_s, chunk).astype(F32)
         r = lax.rsqrt(jnp.mean(xq * xq, -1, keepdims=True) + EPS)
-        qn_s[chunk * width:(chunk + 1) * width, :] = (xq * r * qg).astype(BF16)
-
-    def gather_step(stream, hop):
-        for way in (0, 1):
-            if hop > HOPS[stream, way]:
+        qn_s[wide(chunk), :] = (xq * r * qg).astype(BF16)
+        return carry
+
+    def gather_step(part, hop):
+        for way in (1, 0):
+            if hop > HOPS[min(part, 1), way]:
                 continue
-            ag[stream, way, hop].wait_recv()
-            if hop < HOPS[stream, way]:
-                ag[stream, way, hop + 1] = gather_send(stream, way, hop + 1)
-            c = c_of(-hop if way == 0 else hop, stream)
-            core_send(c)
-            z_send(c)
+            ag[part, way, hop].wait_recv()
+            if hop < HOPS[min(part, 1), way]:
+                ag[part, way, hop + 1] = gather_send(part, way, hop + 1)
+            c = c_of(-hop if way == 0 else hop, min(part, 1))
+            core_send(c, part)
+            if part != 1:
+                z_send(c)
 
     arrived = 0
 
-    def project(parts):
-        total = jnp.zeros((HD, HD), F32)
-        for part in parts:
-            at = (y // 2 + part) % 4
-            cols = feat_s[:, pl.ds(pl.multiple_of(at * 1920, 1920), 1920)]
-            total += dot(cols, wbuf[pl.ds(4 * at, 4)].reshape(1920, HD))
-        return total
+    def project(part, total):
+        at = (y // 2 + part) % 4
+        cols = feat_s[:, pl.ds(pl.multiple_of(at * 1920, 1920), 1920)]
+        return total + dot(cols, wbuf[pl.ds(4 * at, 4)].reshape(1920, HD))
 
     proj = jnp.zeros((HD, HD), F32)
+    lax.fori_loop(0, 4, transpose_part, 0)
     for hop in range(1, 6):
         if hop <= 4:
-            transpose_part(hop - 1)
             gather_step(0, hop)
         if hop == 1:
-            zcopy.wait_recv()
-            for way in (0, 1):
-                ag[1, way, 1] = gather_send(1, way, 1)
-            core_send(c_of(0, 1))
+            for part in (1, 2):
+                zcopies[part].wait_recv()
+                for way in (1, 0):
+                    ag[part, way, 1] = gather_send(part, way, 1)
+                core_send(c_of(0, 1), part)
             z_send(c_of(0, 1))
+            lax.fori_loop(0, chunks, query_norm, 0)
         else:
             gather_step(1, hop - 1)
-        if hop <= 4:
-            query_norm(hop - 1)
-        if hop >= 3:
-            until, parts = {3: (8, (0,)), 4: (15, (1, 3)), 5: (16, (2,))}[hop]
-            for copy in across[arrived:until]:
+            gather_step(2, hop - 1)
+        if hop >= 4:
+            first_part, end_part = {4: (3, 6), 5: (6, 7)}[hop]
+            for copy in across[arrived:]:
                 copy.wait_recv()
-            arrived = until
-            proj += project(parts)
+            arrived = len(across)
+            proj = lax.fori_loop(first_part, end_part, project, proj)
     own_s[...] = proj.astype(BF16)
     pcopy = send(own_s, par_s, p_ss.at[0], p_rs.at[0], partner)
     copies[4].wait()
-    query_norm(4)
-    query_norm(5)
     lane = lax.broadcasted_iota(jnp.int32, (HD, HD), 1)
     half = lane < 64
     lowf = jnp.where(low, 1.0, 0.0).astype(F32)
@@ -222,10 +243,8 @@
     kg_s[...] = jnp.zeros_like(kg_s)
 
     def attend(chunk, carry):
-        at = pl.ds(pl.multiple_of(chunk * CH, CH), CH)
-        wide = pl.ds(pl.multiple_of(chunk * width, width), width)
-        qn = qn_s[wide, :]
-        do = jnp.concatenate([do_s[at, h * HD:(h + 1) * HD] for h in range(heads)], 0)
+        qn = qn_s[wide(chunk), :]
+        do = stack(do_s, chunk)
         e = jnp.exp(dot(kbf_s[...], qn, NT) * inverse) * live
         p = e * (1.0 / jnp.sum(e, 0, keepdims=True))
         pb = p.astype(BF16)
@@ -233,11 +252,11 @@
         pg = dot(vbf_s[...], do, NT)
         delta = jnp.sum(pb.astype(F32) * pg, 0, keepdims=True)
         ds = (p * (pg - delta)).astype(BF16)
-        dsT[:, wide] = ds
+        dsT[:, wide(chunk)] = ds
         kg_s[...] += dot(ds, qn)
         return carry
 
-    lax.fori_loop(0, tokens // CH, attend, 0, unroll=3)
+    lax.fori_loop(0, chunks, attend, 0, unroll=2)
 
     weighted = kg_s[...] * (inverse * kg)
     key_grad = k_scale * weighted - keys * (
@@ -246,34 +265,39 @@
     value_grad = vg_s[...]
     low_part = jnp.where(half, key_grad, pltpu.roll(value_grad, 64, 1))
     high_part = jnp.where(half, pltpu.roll(key_grad, 64, 1), value_grad)
+    own_grad_s[...] = low_part * lowf + high_part * (1.0 - lowf)
     far_s[...] = (high_part * lowf + low_part * (1.0 - lowf)).astype(BF16)
-    own_grad = low_part * lowf + high_part * (1.0 - lowf)
-    fcopy = send(far_s, farr_s, p_ss.at[1], p_rs.at[1], partner)
-
-    def query_back(chunk):
+    fcopy = send(far_s, farr_s.at[0], p_ss.at[1], p_rs.at[1], partner)
+    ocopy = send(own_grad_s, other_grad_s, c_ss.at[4], c_rs.at[4], far_core)
+    dcopy = send(far_s, farr_s.at[1], p_ss.at[2], p_rs.at[2], diagonal)
+
+    def query_back(chunk, carry):
         xq = stack(q_s, chunk).astype(F32)
         r = lax.rsqrt(jnp.mean(xq * xq, -1, keepdims=True) + EPS)
-        ds = dsT[:, chunk * width:(chunk + 1) * width]
-        u = dot(ds, kbf_s[...], TN) * (inverse * qg)
+        u = dot(dsT[:, wide(chunk)], kbf_s[...], TN) * (inverse * qg)
         m = jnp.mean(u * xq, -1, keepdims=True)
         back = (r * u - xq * (r * r * r * m)).astype(BF16)
+        at = pl.ds(pl.multiple_of(chunk * CH, CH), CH)
         for h in range(heads):
-            dq_s[chunk * CH:(chunk + 1) * CH, h * HD:(h + 1) * HD] = back[h * CH:(h + 1) * CH]
-
-    query_back(0)
+            dq_s[at, h * HD:(h + 1) * HD] = back[h * CH:(h + 1) * CH]
+        return carry
+
+    drain((fcopy, ocopy, dcopy))
+    lax.fori_loop(0, 3, query_back, 0)
+    for part in range(4):
+        shared_copy(part).wait_send()
     fcopy.wait_recv()
-    g4_s[zl] = (own_grad + farr_s[...].astype(F32)).astype(BF16)
+    g4_s[zl] = (own_grad_s[...] + farr_s[0].astype(F32)).astype(BF16)
     g = g4_s[zl]
-    gcopy = send(g4_s.at[zl], go_s, c_ss.at[4], c_rs.at[4], far_core)
     gz = []
     for k in (1, 2, 0):
         gz.append(send(g4_s.at[zl], g4_s.at[zl], gz_ss.at[k], gz_rs.at[k], z_to[k]))
 
-    query_back(1)
-    gcopy.wait_recv()
-    go = go_s[...]
-    for copy in shared:
-        copy.wait_recv()
+    ocopy.wait_recv()
+    dcopy.wait_recv()
+    go = (other_grad_s[...] + farr_s[1].astype(F32)).astype(BF16)
+    for part in range(4):
+        shared_copy(part).wait_recv()
 
     def weight_term(step):
         for stream in (1, 0):
@@ -358,26 +382,23 @@
     ring_send(1, 0, 1)
     weight_term(5)
     ring_send(0, 1, 1)
-    weight_term(2)
-    weight_term(6)
+    def later_terms(j, carry):
+        weight_term(6 + j)
+        return carry
+
+    lax.fori_loop(0, 5, later_terms, 0)
     w2_across()
     ring_hop(2)
-    weight_term(1)
-    weight_term(7)
-    weight_term(0)
     x_start()
     ring_hop(3)
     own_term = feature_term(x)
     x_relay()
-    query_back(2)
-    query_back(3)
     ring_hop(4)
+    lax.fori_loop(3, chunks, query_back, 0)
     for name in ("r2", "l2", "r3", "l3"):
         xs[name].wait_recv()
     own_term += x2_s[0].reshape(480, HD).astype(F32) + x2_s[1].reshape(480, HD).astype(F32)
     ft_s[...] = own_term.astype(BF16)
-    query_back(4)
-    query_back(5)
     outs = [
         pltpu.make_async_copy(dq_s, dq_hbm, loc_sem.at[7]),
         pltpu.make_async_copy(ft_s, ft_hbm, loc_sem.at[8]),
@@ -399,6 +420,10 @@
     hz_s[...] = final_rows(1).astype(BF16)
     hcopy = send(hz_s, hzr_s, h_ss, h_rs, far_z)
     own_rows = final_rows(0)
+    drain((hcopy,))
+    for dz in (1, 2, 3):
+        for i in range(4):
+            z_copy(4 * ((zl + dz) % ZL) + i)[1].wait_send()
     hcopy.wait_recv()
     own_rows += hzr_s[...].astype(F32)
     padded = jnp.concatenate((own_rows, jnp.zeros((256 - rows, HD), F32)), 0)
@@ -407,11 +432,7 @@
     vgw_s[...] = turned[64:, :rows]
     outs[2].start()
     outs[3].start()
-    for dz in (1, 2, 3):
-        for i in range(4):
-            z_copy(4 * ((zl + dz) % ZL) + i)[1].wait_send()
-    for copy in sent:
-        copy.wait_send()
+    drain()
     for copy in outs:
         copy.wait()
 
@@ -457,10 +478,12 @@
         pltpu.VMEM((tokens * q_width // HD, HD), BF16),
         pltpu.VMEM((ZL, X, 2) + piece, BF16),
     ]
-    scratch += [pltpu.VMEM((HD, HD), BF16)] * 6
+    scratch += [pltpu.VMEM((HD, HD), BF16)] * 5
     scratch += [
+        pltpu.VMEM((2, HD, HD), BF16),
         pltpu.VMEM((ZL, HD, HD), BF16),
-        pltpu.VMEM((HD, HD), BF16),
+        pltpu.VMEM((HD, HD), F32),
+        pltpu.VMEM((HD, HD), F32),
         pltpu.VMEM((X, 2) + piece, BF16),
         pltpu.VMEM((16,) + piece, BF16),
         pltpu.VMEM((16,) + piece, BF16),
@@ -479,7 +502,7 @@
         pltpu.VMEM((column_half, rows), F32),
         pltpu.VMEM((column_half, rows), F32),
         dma((11,)),
-        dma((2, 2, 4)), dma((2, 2, 4)), dma, dma, dma((16,)), dma((16,)), dma((2,)), dma((2,)),
+        dma((3, 2, 4)), dma((3, 2, 4)), dma((2,)), dma((2,)), dma((24,)), dma((24,)), dma((3,)), dma((3,)),
         dma((8,)), dma((8,)), dma((14,)), dma((14,)), dma((6,)), dma((6,)),
         dma((16,)), dma((4, 4)), dma((3, 4)), dma((3, 4)), dma((3,)), dma((3,)), dma, dma,
     ]

time: 74.5 us -> 71.6 us (0.961)
  the two profiles are of different devices: /device:TPU:128 before, /device:TPU:136 now
where the time goes in v4:
time: 71.6 us; the launch traced here: 71.4 us
  Pallas kernels  70.2 us (98%)
  between operations  1.29 us (2%)
    pallas_call x1, Pallas kernels, shards(): pl.pallas_call(kernel, out_shape=out_shape, in_specs=[pl.BlockSpec(memory...  68 us
    pallas_call x1, Pallas kernels, shards(): pl.pallas_call(copy_out, out_shape=out_shape, in_specs=[anyspec] * 4, out...  2.21 us

profile of v4, /device:TPU:136, one launch (start us, length us, event | category | flops | bytes accessed | tf_op | source)
XLA Modules:
  0.0 71.4 jit_solution(8632956572970724108)
XLA Ops:
  1.3 68.0 %shard_map.111 = (bf16[960,512]{1,0:T(8,128)(2,1)}, bf16[480,128]{1,0:T(8,128)(2,1)}, f32[64,240]{1,0:T(8,128)}, f32[64,240]{1,0:T(8,128)}) custom-call(s32[1]{0:T(128)S(6)} %copy.12.tc_ref, bf16[960,512]{1,0:T(8,128)(2,1)} %q_hbm.1, bf16[128,7680]{1,0:T(8,128)(2,1)} %bitcast.10, bf16[64,240]{1,0:T(8,128)(2,1)} %bitcast.14, bf16[64,240]{1,0:T(8,128)(2,1)} %bitcast.15, ...), custom_call_target="tpu_custom_call" | custom-call | flops 1600000000 | bytes 8000000 | tf_op jit(solution)/shard_map/pallas_call | solution.py:515
  69.2 2.2 %shard_map.112 = (bf16[960,512]{1,0:T(8,128)(2,1)}, bf16[480,128]{1,0:T(8,128)(2,1)}, f32[64,240]{1,0:T(8,128)}, f32[64,240]{1,0:T(8,128)}) custom-call(bf16[960,512]{1,0:T(8,128)(2,1)} %get-tuple-element.12.a, bf16[480,128]{1,0:T(8,128)(2,1)} %get-tuple-element.13.b, f32[64,240]{1,0:T(8,128)} %get-tuple-element.14.c, f32[64,240]{1,0:T(8,128)} %get-tuple-element.15.e), custom_call_target="tpu_custom_call" | custom-call | bytes 3000000 | tf_op jit(solution)/shard_map/pallas_call | solution.py:531

commit v5 on v4

--- a/solution.py
+++ b/solution.py
@@ -135,14 +135,13 @@
             copy.start()
 
     ag = {}
-    for way in (0, 1):
-        ag[0, way, 1] = gather_send(0, way, 1)
     zcopies = {}
     for part in (1, 2):
         ref = piece_of(mine, part)
         zcopies[part] = send(ref, ref, agz_ss.at[part - 1], agz_rs.at[part - 1], far_z)
+    for way in (0, 1):
+        ag[0, way, 1] = gather_send(0, way, 1)
     core_send(mine, 0)
-    z_send(mine)
 
     copies[2].wait()
     copies[3].wait()
@@ -188,10 +187,11 @@
                 ag[part, way, hop + 1] = gather_send(part, way, hop + 1)
             c = c_of(-hop if way == 0 else hop, min(part, 1))
             core_send(c, part)
-            if part != 1:
+            if part == 2 or (part == 0 and hop > 1):
                 z_send(c)
 
     arrived = 0
+    marks = []
 
     def project(part, total):
         at = (y // 2 + part) % 4
@@ -199,7 +199,6 @@
         return total + dot(cols, wbuf[pl.ds(4 * at, 4)].reshape(1920, HD))
 
     proj = jnp.zeros((HD, HD), F32)
-    lax.fori_loop(0, 4, transpose_part, 0)
     for hop in range(1, 6):
         if hop <= 4:
             gather_step(0, hop)
@@ -209,20 +208,26 @@
                 for way in (1, 0):
                     ag[part, way, 1] = gather_send(part, way, 1)
                 core_send(c_of(0, 1), part)
-            z_send(c_of(0, 1))
-            lax.fori_loop(0, chunks, query_norm, 0)
+            for c in (mine, c_of(-1, 0), c_of(1, 0), c_of(0, 1)):
+                z_send(c)
         else:
             gather_step(1, hop - 1)
             gather_step(2, hop - 1)
+        if hop <= 4:
+            transpose_part(hop - 1, 0)
+            query_norm(hop - 1, 0)
+        marks.append(len(across))
         if hop >= 4:
-            first_part, end_part = {4: (3, 6), 5: (6, 7)}[hop]
-            for copy in across[arrived:]:
-                copy.wait_recv()
-            arrived = len(across)
-            proj = lax.fori_loop(first_part, end_part, project, proj)
+            for mark, first_part, end_part in {4: ((2, 4, 5),), 5: ((3, 5, 6), (3, 7, 8), (4, 6, 7))}[hop]:
+                for copy in across[arrived:marks[mark]]:
+                    copy.wait_recv()
+                arrived = max(arrived, marks[mark])
+                for part in range(first_part, end_part):
+                    proj = project(part, proj)
     own_s[...] = proj.astype(BF16)
     pcopy = send(own_s, par_s, p_ss.at[0], p_rs.at[0], partner)
     copies[4].wait()
+    lax.fori_loop(4, chunks, query_norm, 0)
     lane = lax.broadcasted_iota(jnp.int32, (HD, HD), 1)
     half = lane < 64
     lowf = jnp.where(low, 1.0, 0.0).astype(F32)
@@ -375,6 +380,15 @@
             if hop <= HOPS[stream, way]:
                 ring_send(stream, way, hop)
 
+    def final_rows(stream):
+        c = c_of(0, stream)
+        total = wterm[c].astype(F32)
+        for way in (0, 1):
+            hop = HOPS[stream, way]
+            ys[stream, way, hop].wait_recv()
+            total += yr_s[slots[stream, way, hop]].astype(F32)
+        return total
+
     weight_term(4)
     ring_send(1, 1, 1)
     ring_send(0, 0, 1)
@@ -387,13 +401,15 @@
         return carry
 
     lax.fori_loop(0, 5, later_terms, 0)
+    ring_hop(2)
     w2_across()
-    ring_hop(2)
+    ring_hop(3)
     x_start()
-    ring_hop(3)
+    ring_hop(4)
+    x_relay()
+    hz_s[...] = final_rows(1).astype(BF16)
+    hcopy = send(hz_s, hzr_s, h_ss, h_rs, far_z)
     own_term = feature_term(x)
-    x_relay()
-    ring_hop(4)
     lax.fori_loop(3, chunks, query_back, 0)
     for name in ("r2", "l2", "r3", "l3"):
         xs[name].wait_recv()
@@ -408,17 +424,6 @@
     outs[0].start()
     outs[1].start()
 
-    def final_rows(stream):
-        c = c_of(0, stream)
-        total = wterm[c].astype(F32)
-        for way in (0, 1):
-            hop = HOPS[stream, way]
-            ys[stream, way, hop].wait_recv()
-            total += yr_s[slots[stream, way, hop]].astype(F32)
-        return total
-
-    hz_s[...] = final_rows(1).astype(BF16)
-    hcopy = send(hz_s, hzr_s, h_ss, h_rs, far_z)
     own_rows = final_rows(0)
     drain((hcopy,))
     for dz in (1, 2, 3):

time: 71.6 us -> 70.1 us (0.979)
  the two profiles are of different devices: /device:TPU:136 before, /device:TPU:8 now
where the time goes in v5:
time: 70.1 us; the launch traced here: 69.9 us
  Pallas kernels  68.7 us (98%)
  between operations  1.29 us (2%)
    pallas_call x1, Pallas kernels, shards(): pl.pallas_call(kernel, out_shape=out_shape, in_specs=[pl.BlockSpec(memory...  66.5 us
    pallas_call x1, Pallas kernels, shards(): pl.pallas_call(copy_out, out_shape=out_shape, in_specs=[anyspec] * 4, out...  2.21 us

profile of v5, /device:TPU:8, one launch (start us, length us, event | category | flops | bytes accessed | tf_op | source)
XLA Modules:
  0.0 69.9 jit_solution(18237949467117590662)
XLA Ops:
  1.3 66.5 %shard_map.111 = (bf16[960,512]{1,0:T(8,128)(2,1)}, bf16[480,128]{1,0:T(8,128)(2,1)}, f32[64,240]{1,0:T(8,128)}, f32[64,240]{1,0:T(8,128)}) custom-call(s32[1]{0:T(128)S(6)} %copy.12.tc_ref, bf16[960,512]{1,0:T(8,128)(2,1)} %q_hbm.1, bf16[128,7680]{1,0:T(8,128)(2,1)} %bitcast.10, bf16[64,240]{1,0:T(8,128)(2,1)} %bitcast.14, bf16[64,240]{1,0:T(8,128)(2,1)} %bitcast.15, ...), custom_call_target="tpu_custom_call" | custom-call | flops 1600000000 | bytes 8000000 | tf_op jit(solution)/shard_map/pallas_call | solution.py:520
  67.7 2.2 %shard_map.112 = (bf16[960,512]{1,0:T(8,128)(2,1)}, bf16[480,128]{1,0:T(8,128)(2,1)}, f32[64,240]{1,0:T(8,128)}, f32[64,240]{1,0:T(8,128)}) custom-call(bf16[960,512]{1,0:T(8,128)(2,1)} %get-tuple-element.12.a, bf16[480,128]{1,0:T(8,128)(2,1)} %get-tuple-element.13.b, f32[64,240]{1,0:T(8,128)} %get-tuple-element.14.c, f32[64,240]{1,0:T(8,128)} %get-tuple-element.15.e), custom_call_target="tpu_custom_call" | custom-call | bytes 3000000 | tf_op jit(solution)/shard_map/pallas_call | solution.py:536

commit v6 on v5

--- a/solution.py
+++ b/solution.py
@@ -162,7 +162,6 @@
     def transpose_part(part, carry):
         cols = feat_s[:, pl.ds(pl.multiple_of(part * 1920, 1920), 1920)]
         featT[pl.ds(part * 4, 4)] = jnp.transpose(cols).reshape(4, 2, 240, HD)
-        shared_copy(part).start()
         return carry
 
     def stack(ref, chunk):
@@ -226,6 +225,8 @@
                     proj = project(part, proj)
     own_s[...] = proj.astype(BF16)
     pcopy = send(own_s, par_s, p_ss.at[0], p_rs.at[0], partner)
+    for part in range(4):
+        shared_copy(part).start()
     copies[4].wait()
     lax.fori_loop(4, chunks, query_norm, 0)
     lane = lax.broadcasted_iota(jnp.int32, (HD, HD), 1)

time: 70.1 us -> 70.1 us (level)
  no operation moved by 1% of the time
where the time goes in v6:
time: 70.1 us; the launch traced here: 69.9 us
  Pallas kernels  68.7 us (98%)
  between operations  1.29 us (2%)
    pallas_call x1, Pallas kernels, shards(): pl.pallas_call(kernel, out_shape=out_shape, in_specs=[pl.BlockSpec(memory...  66.4 us
    pallas_call x1, Pallas kernels, shards(): pl.pallas_call(copy_out, out_shape=out_shape, in_specs=[anyspec] * 4, out...  2.21 us

profile of v6, /device:TPU:8, one launch (start us, length us, event | category | flops | bytes accessed | tf_op | source)
XLA Modules:
  0.0 69.9 jit_solution(6029254669588999579)
XLA Ops:
  1.3 66.4 %shard_map.111 = (bf16[960,512]{1,0:T(8,128)(2,1)}, bf16[480,128]{1,0:T(8,128)(2,1)}, f32[64,240]{1,0:T(8,128)}, f32[64,240]{1,0:T(8,128)}) custom-call(s32[1]{0:T(128)S(6)} %copy.12.tc_ref, bf16[960,512]{1,0:T(8,128)(2,1)} %q_hbm.1, bf16[128,7680]{1,0:T(8,128)(2,1)} %bitcast.10, bf16[64,240]{1,0:T(8,128)(2,1)} %bitcast.14, bf16[64,240]{1,0:T(8,128)(2,1)} %bitcast.15, ...), custom_call_target="tpu_custom_call" | custom-call | flops 1600000000 | bytes 8000000 | tf_op jit(solution)/shard_map/pallas_call | solution.py:521
  67.7 2.2 %shard_map.112 = (bf16[960,512]{1,0:T(8,128)(2,1)}, bf16[480,128]{1,0:T(8,128)(2,1)}, f32[64,240]{1,0:T(8,128)}, f32[64,240]{1,0:T(8,128)}) custom-call(bf16[960,512]{1,0:T(8,128)(2,1)} %get-tuple-element.12.a, bf16[480,128]{1,0:T(8,128)(2,1)} %get-tuple-element.13.b, f32[64,240]{1,0:T(8,128)} %get-tuple-element.14.c, f32[64,240]{1,0:T(8,128)} %get-tuple-element.15.e), custom_call_target="tpu_custom_call" | custom-call | bytes 3000000 | tf_op jit(solution)/shard_map/pallas_call | solution.py:537

commit v7 on v6

--- a/solution.py
+++ b/solution.py
@@ -350,23 +350,34 @@
                 wc.append(send(ref, ref, wc_ss.at[dz - 1, i], wc_rs.at[dz - 1, i], far_core))
 
     slots = {}
-    for key in ((0, 0), (1, 1), (0, 1), (1, 0)):
-        for hop in range(1, HOPS[key] + 1):
-            slots[key + (hop,)] = len(slots)
+    for part in range(3):
+        for way in (0, 1):
+            for hop in range(1, HOPS[min(part, 1), way] + 1):
+                slots[part, way, hop] = len(slots)
     ys = {}
 
-    def ring_send(stream, way, hop):
+    def ring_send(part, way, hop):
+        stream = min(part, 1)
         step = HOPS[stream, way] - hop + 1
         c = c_of(step if way == 0 else -step, stream)
-        slot = slots[stream, way, hop]
+        slot = slots[part, way, hop]
+        at = pl.ds(*PIECES[part])
+        count = PIECES[part][1]
         if hop > 1:
-            ys[stream, way, hop - 1].wait_recv()
-            last = slots[stream, way, hop - 1]
-            wterm[c] = (wterm[c].astype(F32) + yr_s[last].astype(F32)).astype(BF16)
-        ys[stream, way, hop] = send(
-            wterm.at[c], yr_s.at[slot], y_ss.at[slot], y_rs.at[slot],
+            ys[part, way, hop - 1].wait_recv()
+            last = slots[part, way, hop - 1]
+            wterm[c, at] = (
+                wterm[c, at].astype(F32) + yr_s[last, :count].astype(F32)
+            ).astype(BF16)
+        ys[part, way, hop] = send(
+            wterm.at[c, at], yr_s.at[slot, pl.ds(0, count)], y_ss.at[slot], y_rs.at[slot],
             right if way == 0 else left,
         )
+
+    def ring_hop(hop):
+        for part, way in ((1, 1), (1, 0), (2, 1), (2, 0), (0, 0), (0, 1)):
+            if hop <= HOPS[min(part, 1), way]:
+                ring_send(part, way, hop)
 
     def x_relay():
         for name, way, xx in (("r", 0, xp), ("l", 1, xm)):
@@ -376,27 +387,25 @@
             x_send(name + "3", 4 + way, fterm.at[xx, way], x2_s.at[way, way],
                    x_right if way == 0 else x_left)
 
-    def ring_hop(hop):
-        for stream, way in ((1, 1), (1, 0), (0, 0), (0, 1)):
-            if hop <= HOPS[stream, way]:
-                ring_send(stream, way, hop)
-
-    def final_rows(stream):
-        c = c_of(0, stream)
-        total = wterm[c].astype(F32)
+    def final_rows(part):
+        at = pl.ds(*PIECES[part])
+        total = wterm[c_of(0, min(part, 1)), at].astype(F32)
         for way in (0, 1):
-            hop = HOPS[stream, way]
-            ys[stream, way, hop].wait_recv()
-            total += yr_s[slots[stream, way, hop]].astype(F32)
+            last = part, way, HOPS[min(part, 1), way]
+            ys[last].wait_recv()
+            total += yr_s[slots[last], :PIECES[part][1]].astype(F32)
         return total
 
     weight_term(4)
     ring_send(1, 1, 1)
+    ring_send(2, 1, 1)
     ring_send(0, 0, 1)
     weight_term(3)
     ring_send(1, 0, 1)
+    ring_send(2, 0, 1)
     weight_term(5)
     ring_send(0, 1, 1)
+
     def later_terms(j, carry):
         weight_term(6 + j)
         return carry
@@ -408,8 +417,12 @@
     x_start()
     ring_hop(4)
     x_relay()
-    hz_s[...] = final_rows(1).astype(BF16)
-    hcopy = send(hz_s, hzr_s, h_ss, h_rs, far_z)
+    hcopies = []
+    for part in (1, 2):
+        at = pl.ds(*PIECES[part])
+        hz_s[at] = final_rows(part).astype(BF16)
+        hcopies.append(
+            send(hz_s.at[at], hzr_s.at[at], h_ss.at[part - 1], h_rs.at[part - 1], far_z))
     own_term = feature_term(x)
     lax.fori_loop(3, chunks, query_back, 0)
     for name in ("r2", "l2", "r3", "l3"):
@@ -426,11 +439,12 @@
     outs[1].start()
 
     own_rows = final_rows(0)
-    drain((hcopy,))
+    drain(hcopies)
     for dz in (1, 2, 3):
         for i in range(4):
             z_copy(4 * ((zl + dz) % ZL) + i)[1].wait_send()
-    hcopy.wait_recv()
+    for copy in hcopies:
+        copy.wait_recv()
     own_rows += hzr_s[...].astype(F32)
     padded = jnp.concatenate((own_rows, jnp.zeros((256 - rows, HD), F32)), 0)
     turned = jnp.transpose(padded)
@@ -493,7 +507,7 @@
         pltpu.VMEM((X, 2) + piece, BF16),
         pltpu.VMEM((16,) + piece, BF16),
         pltpu.VMEM((16,) + piece, BF16),
-        pltpu.VMEM((14,) + piece, BF16),
+        pltpu.VMEM((21,) + piece, BF16),
         pltpu.VMEM((2,) + piece, BF16),
         pltpu.VMEM((2, 2) + piece, BF16),
         pltpu.VMEM(piece, BF16),
@@ -509,8 +523,8 @@
         pltpu.VMEM((column_half, rows), F32),
         dma((11,)),
         dma((3, 2, 4)), dma((3, 2, 4)), dma((2,)), dma((2,)), dma((24,)), dma((24,)), dma((3,)), dma((3,)),
-        dma((8,)), dma((8,)), dma((14,)), dma((14,)), dma((6,)), dma((6,)),
-        dma((16,)), dma((4, 4)), dma((3, 4)), dma((3, 4)), dma((3,)), dma((3,)), dma, dma,
+        dma((8,)), dma((8,)), dma((21,)), dma((21,)), dma((6,)), dma((6,)),
+        dma((16,)), dma((4, 4)), dma((3, 4)), dma((3, 4)), dma((3,)), dma((3,)), dma((2,)), dma((2,)),
     ]
     out_shape = (
         jax.ShapeDtypeStruct((tokens, q_width), BF16),

time: 70.1 us -> 69.9 us (level)
  no operation moved by 1% of the time
where the time goes in v7:
time: 69.9 us; the launch traced here: 69.7 us
  Pallas kernels  68.4 us (98%)
  between operations  1.29 us (2%)
    pallas_call x1, Pallas kernels, shards(): pl.pallas_call(kernel, out_shape=out_shape, in_specs=[pl.BlockSpec(memory...  66.2 us
    pallas_call x1, Pallas kernels, shards(): pl.pallas_call(copy_out, out_shape=out_shape, in_specs=[anyspec] * 4, out...  2.21 us

profile of v7, /device:TPU:8, one launch (start us, length us, event | category | flops | bytes accessed | tf_op | source)
XLA Modules:
  0.0 69.7 jit_solution(10366322891686872645)
XLA Ops:
  1.3 66.2 %shard_map.111 = (bf16[960,512]{1,0:T(8,128)(2,1)}, bf16[480,128]{1,0:T(8,128)(2,1)}, f32[64,240]{1,0:T(8,128)}, f32[64,240]{1,0:T(8,128)}) custom-call(s32[1]{0:T(128)S(6)} %copy.12.tc_ref, bf16[960,512]{1,0:T(8,128)(2,1)} %q_hbm.1, bf16[128,7680]{1,0:T(8,128)(2,1)} %bitcast.10, bf16[64,240]{1,0:T(8,128)(2,1)} %bitcast.14, bf16[64,240]{1,0:T(8,128)(2,1)} %bitcast.15, ...), custom_call_target="tpu_custom_call" | custom-call | flops 1600000000 | bytes 8000000 | tf_op jit(solution)/shard_map/pallas_call | solution.py:535
  67.5 2.2 %shard_map.112 = (bf16[960,512]{1,0:T(8,128)(2,1)}, bf16[480,128]{1,0:T(8,128)(2,1)}, f32[64,240]{1,0:T(8,128)}, f32[64,240]{1,0:T(8,128)}) custom-call(bf16[960,512]{1,0:T(8,128)(2,1)} %get-tuple-element.12.a, bf16[480,128]{1,0:T(8,128)(2,1)} %get-tuple-element.13.b, f32[64,240]{1,0:T(8,128)} %get-tuple-element.14.c, f32[64,240]{1,0:T(8,128)} %get-tuple-element.15.e), custom_call_target="tpu_custom_call" | custom-call | bytes 3000000 | tf_op jit(solution)/shard_map/pallas_call | solution.py:551

commit v8 on v7

--- a/solution.py
+++ b/solution.py
@@ -262,7 +262,7 @@
         kg_s[...] += dot(ds, qn)
         return carry
 
-    lax.fori_loop(0, chunks, attend, 0, unroll=2)
+    lax.fori_loop(0, chunks, attend, 0, unroll=3)
 
     weighted = kg_s[...] * (inverse * kg)
     key_grad = k_scale * weighted - keys * (
@@ -412,17 +412,17 @@
 
     lax.fori_loop(0, 5, later_terms, 0)
     ring_hop(2)
+    ring_hop(3)
     w2_across()
-    ring_hop(3)
+    ring_hop(4)
     x_start()
-    ring_hop(4)
-    x_relay()
     hcopies = []
     for part in (1, 2):
         at = pl.ds(*PIECES[part])
         hz_s[at] = final_rows(part).astype(BF16)
         hcopies.append(
             send(hz_s.at[at], hzr_s.at[at], h_ss.at[part - 1], h_rs.at[part - 1], far_z))
+    x_relay()
     own_term = feature_term(x)
     lax.fori_loop(3, chunks, query_back, 0)
     for name in ("r2", "l2", "r3", "l3"):

time: 69.9 us -> 70.7 us (1.011)
  the two profiles are of different devices: /device:TPU:8 before, /device:TPU:2 now
where the time goes in v8:
time: 70.7 us; the launch traced here: 70.6 us
  Pallas kernels  69.3 us (98%)
  between operations  1.29 us (2%)
    pallas_call x1, Pallas kernels, shards(): pl.pallas_call(kernel, out_shape=out_shape, in_specs=[pl.BlockSpec(memory...  67.1 us
    pallas_call x1, Pallas kernels, shards(): pl.pallas_call(copy_out, out_shape=out_shape, in_specs=[anyspec] * 4, out...  2.21 us

profile of v8, /device:TPU:2, one launch (start us, length us, event | category | flops | bytes accessed | tf_op | source)
XLA Modules:
  0.0 70.6 jit_solution(18114535059633190038)
XLA Ops:
  1.3 67.1 %shard_map.111 = (bf16[960,512]{1,0:T(8,128)(2,1)}, bf16[480,128]{1,0:T(8,128)(2,1)}, f32[64,240]{1,0:T(8,128)}, f32[64,240]{1,0:T(8,128)}) custom-call(s32[1]{0:T(128)S(6)} %copy.12.tc_ref, bf16[960,512]{1,0:T(8,128)(2,1)} %q_hbm.1, bf16[128,7680]{1,0:T(8,128)(2,1)} %bitcast.10, bf16[64,240]{1,0:T(8,128)(2,1)} %bitcast.14, bf16[64,240]{1,0:T(8,128)(2,1)} %bitcast.15, ...), custom_call_target="tpu_custom_call" | custom-call | flops 1600000000 | bytes 8000000 | tf_op jit(solution)/shard_map/pallas_call | solution.py:535
  68.4 2.2 %shard_map.112 = (bf16[960,512]{1,0:T(8,128)(2,1)}, bf16[480,128]{1,0:T(8,128)(2,1)}, f32[64,240]{1,0:T(8,128)}, f32[64,240]{1,0:T(8,128)}) custom-call(bf16[960,512]{1,0:T(8,128)(2,1)} %get-tuple-element.12.a, bf16[480,128]{1,0:T(8,128)(2,1)} %get-tuple-element.13.b, f32[64,240]{1,0:T(8,128)} %get-tuple-element.14.c, f32[64,240]{1,0:T(8,128)} %get-tuple-element.15.e), custom_call_target="tpu_custom_call" | custom-call | bytes 3000000 | tf_op jit(solution)/shard_map/pallas_call | solution.py:551

commit v9 on v8

--- a/solution.py
+++ b/solution.py
@@ -187,10 +187,14 @@
             c = c_of(-hop if way == 0 else hop, min(part, 1))
             core_send(c, part)
             if part == 2 or (part == 0 and hop > 1):
-                z_send(c)
+                if hop <= 2:
+                    z_send(c)
+                else:
+                    z_later.append(c)
 
     arrived = 0
     marks = []
+    z_later = []
 
     def project(part, total):
         at = (y // 2 + part) % 4
@@ -225,6 +229,8 @@
                     proj = project(part, proj)
     own_s[...] = proj.astype(BF16)
     pcopy = send(own_s, par_s, p_ss.at[0], p_rs.at[0], partner)
+    for c in z_later:
+        z_send(c)
     for part in range(4):
         shared_copy(part).start()
     copies[4].wait()

time: 70.7 us -> 70.5 us (level)
  the two profiles are of different devices: /device:TPU:2 before, /device:TPU:64 now
where the time goes in v9:
time: 70.5 us; the launch traced here: 70.3 us
  Pallas kernels  69 us (98%)
  between operations  1.29 us (2%)
    pallas_call x1, Pallas kernels, shards(): pl.pallas_call(kernel, out_shape=out_shape, in_specs=[pl.BlockSpec(memory...  66.8 us
    pallas_call x1, Pallas kernels, shards(): pl.pallas_call(copy_out, out_shape=out_shape, in_specs=[anyspec] * 4, out...  2.21 us

profile of v9, /device:TPU:64, one launch (start us, length us, event | category | flops | bytes accessed | tf_op | source)
XLA Modules:
  0.0 70.3 jit_solution(9116349488199467527)
XLA Ops:
  1.3 66.8 %shard_map.111 = (bf16[960,512]{1,0:T(8,128)(2,1)}, bf16[480,128]{1,0:T(8,128)(2,1)}, f32[64,240]{1,0:T(8,128)}, f32[64,240]{1,0:T(8,128)}) custom-call(s32[1]{0:T(128)S(6)} %copy.12.tc_ref, bf16[960,512]{1,0:T(8,128)(2,1)} %q_hbm.1, bf16[128,7680]{1,0:T(8,128)(2,1)} %bitcast.10, bf16[64,240]{1,0:T(8,128)(2,1)} %bitcast.14, bf16[64,240]{1,0:T(8,128)(2,1)} %bitcast.15, ...), custom_call_target="tpu_custom_call" | custom-call | flops 1600000000 | bytes 8000000 | tf_op jit(solution)/shard_map/pallas_call | solution.py:541
  68.1 2.2 %shard_map.112 = (bf16[960,512]{1,0:T(8,128)(2,1)}, bf16[480,128]{1,0:T(8,128)(2,1)}, f32[64,240]{1,0:T(8,128)}, f32[64,240]{1,0:T(8,128)}) custom-call(bf16[960,512]{1,0:T(8,128)(2,1)} %get-tuple-element.12.a, bf16[480,128]{1,0:T(8,128)(2,1)} %get-tuple-element.13.b, f32[64,240]{1,0:T(8,128)} %get-tuple-element.14.c, f32[64,240]{1,0:T(8,128)} %get-tuple-element.15.e), custom_call_target="tpu_custom_call" | custom-call | bytes 3000000 | tf_op jit(solution)/shard_map/pallas_call | solution.py:557
